TPU v7x, 128 devices: a whole 4x4x4 slice. The times are simulated.
128 devices in a mesh: coarse: 4 (over y_lo, core), sector: 32 (over y_hi, x, z).
Axes of the slice: x: 4, y: 4 (y_hi: 2, y_lo: 2; y = y_hi * 2 + y_lo), z: 4, core: 2. Of those that a mesh axis runs over, the one named last changes fastest.
Arguments:
- fine_populations: float32 [19, 128, 512, 128], P(None, 'coarse', 'sector'), as said below
- coarse_face: float32 [2, 19, 16384], P(None, None, ('coarse', 'sector')), as said below
- ghost_map: int32 [128, 512], P('coarse', 'sector'), may hold values from 0 to 255, as said below
- marker_force: bfloat16 [4096, 3, 128], P(('coarse', 'sector')), may hold values from -6 to 6
- marker_weights: bfloat16 [4096, 128, 128], P(('coarse', 'sector')), may hold values from 0 to 0.015625
- marker_tiles: int32 [4096], P(('coarse', 'sector')), may hold values from 0 to 575, as said below
- block_counts: int32 [128], P(('coarse', 'sector')), may hold values from 4 to 32, as said below
Outputs:
- fine_state: float32 [19, 128, 512, 128], P(None, 'coarse', 'sector')
Inputs may be any that keep to these rules, and one draw needn't show every extreme that they name: `fine_populations`: each population is its lattice weight w_i times a factor between 0.5 and 2. `coarse_face`: each population is its lattice weight w_i times a factor between 0.5 and 2. `ghost_map`: an index into the 128 coarse interface cells of the same device followed by the 128 of the next device along sector, the last device's next being the first. `marker_tiles`: a tile of the block's own device, possibly lying one cell past either azimuthal end of its cells. `block_counts`: some device has all 32 blocks live.
All inputs are finite; a program needn't handle non-finite values.
Results may differ from a plain program's by a relative error of at most 0.0003.
Values sent between devices are 32-bit elements; how exact they have to be, the bound alone decides.
A program may use at most 64 MiB of HBM per device.

v0:
```python
import jax
import jax.numpy as jnp
from jax import lax
from jax.sharding import PartitionSpec as P

VELOCITIES = (
    (0, 0, 0),
    (1, 0, 0),
    (-1, 0, 0),
    (0, 1, 0),
    (0, -1, 0),
    (0, 0, 1),
    (0, 0, -1),
    (1, 1, 0),
    (-1, -1, 0),
    (1, -1, 0),
    (-1, 1, 0),
    (1, 0, 1),
    (-1, 0, -1),
    (1, 0, -1),
    (-1, 0, 1),
    (0, 1, 1),
    (0, -1, -1),
    (0, 1, -1),
    (0, -1, 1),
)
LATTICE_WEIGHTS = (1.0 / 3.0,) + (1.0 / 18.0,) * 6 + (1.0 / 36.0,) * 12
TAU_FINE = 0.8
TAU_COARSE = 0.65
FORCE_FACTOR = 1.0 - 0.5 / TAU_FINE
RESCALE = TAU_FINE / (2.0 * TAU_COARSE)


def extended(cells, sides, width, closed):
    for axis, dim in sides:
        count = lax.axis_size(axis)
        ends = count if closed else count - 1
        head = lax.slice_in_dim(cells, 0, width, axis=dim)
        tail = lax.slice_in_dim(cells, cells.shape[dim] - width, cells.shape[dim], axis=dim)
        cells = jnp.concatenate(
            [
                lax.ppermute(tail, axis, [(i, (i + 1) % count) for i in range(ends)]),
                cells,
                lax.ppermute(head, axis, [((i + 1) % count, i) for i in range(ends)]),
            ],
            axis=dim,
        )
    return cells


def passed_along(value, axis, steps):
    count = lax.axis_size(axis)
    pairs = [(source, (source + steps) % count) for source in range(count)]
    return lax.ppermute(value, axis, pairs)


def opposite(pop_index):
    if pop_index == 0:
        return 0
    return pop_index + 1 if pop_index % 2 == 1 else pop_index - 1


def project(vector, pop_index):
    running = jnp.zeros_like(vector[0])
    for axis_index in range(3):
        component = VELOCITIES[pop_index][axis_index]
        if component == 1:
            running = running + vector[axis_index]
        elif component == -1:
            running = running - vector[axis_index]
    return running


def moments(populations):
    density = populations[0]
    for pop_index in range(1, 19):
        density = density + populations[pop_index]
    momentum = []
    for axis_index in range(3):
        running = jnp.zeros_like(density)
        for pop_index in range(19):
            component = VELOCITIES[pop_index][axis_index]
            if component == 1:
                running = running + populations[pop_index]
            elif component == -1:
                running = running - populations[pop_index]
        momentum.append(running)
    return (density, momentum)


def collide(populations, force_field):
    density, momentum = moments(populations)
    velocity = [
        (momentum[axis_index] + 0.5 * force_field[axis_index]) / density for axis_index in range(3)
    ]
    speed_sq = velocity[0] * velocity[0] + velocity[1] * velocity[1] + velocity[2] * velocity[2]
    along_force = (
        velocity[0] * force_field[0] + velocity[1] * force_field[1] + velocity[2] * force_field[2]
    )
    results = []
    for pop_index in range(19):
        dotted = project(velocity, pop_index)
        pushed = project([force_field[0], force_field[1], force_field[2]], pop_index)
        weight = LATTICE_WEIGHTS[pop_index]
        balance = weight * density * (1.0 + 3.0 * dotted + 4.5 * dotted * dotted - 1.5 * speed_sq)
        source = FORCE_FACTOR * weight * (3.0 * (pushed - along_force) + 9.0 * dotted * pushed)
        results.append(
            populations[pop_index] - (populations[pop_index] - balance) / TAU_FINE + source
        )
    return jnp.stack(results)


def interface_values(coarse_pops):
    density, momentum = moments(coarse_pops)
    velocity = [momentum[axis_index] / density for axis_index in range(3)]
    speed_sq = velocity[0] * velocity[0] + velocity[1] * velocity[1] + velocity[2] * velocity[2]
    results = []
    for pop_index in range(19):
        dotted = project(velocity, pop_index)
        weight = LATTICE_WEIGHTS[pop_index]
        balance = weight * density * (1.0 + 3.0 * dotted + 4.5 * dotted * dotted - 1.5 * speed_sq)
        results.append(balance + RESCALE * (coarse_pops[pop_index] - balance))
    return jnp.stack(results)


def spread_markers(
    marker_force, marker_weights, marker_tiles, block_counts, cells_axial, cells_cycle, cells_radial
):
    blocks = marker_force.shape[0]
    contrib = jnp.einsum(
        "bkm,bmx->bkx", marker_force, marker_weights, preferred_element_type=jnp.float32
    )
    live_mask = jnp.arange(blocks) < block_counts[0]
    contrib = jnp.where(live_mask[:, None, None], contrib, 0.0)
    tiles_cycle = cells_cycle + 2
    buffer = jnp.zeros((3, cells_axial * tiles_cycle, cells_radial), jnp.float32)
    buffer = buffer.at[:, marker_tiles, :].add(jnp.transpose(contrib, (1, 0, 2)))
    buffer = buffer.reshape(3, cells_axial, tiles_cycle, cells_radial)
    rim_pair = jnp.concatenate([buffer[:, :, :1], buffer[:, :, -1:]], axis=2)
    arrived = extended(rim_pair, (("sector", 2),), 1, True)
    force_field = buffer[:, :, 1:-1]
    force_field = force_field.at[:, :, :1].add(arrived[:, :, :1])
    force_field = force_field.at[:, :, -1:].add(arrived[:, :, -1:])
    return force_field


def stream(relaxed, ghost_pops):
    cells_axial, cells_cycle, cells_radial = relaxed.shape[1:]
    cycle_ext = extended(relaxed, (("sector", 2),), 1, True)
    full_ext = extended(cycle_ext, (("coarse", 1),), 1, False)

    def source(pop_index):
        step_axial, step_cycle, step_radial = VELOCITIES[pop_index]
        return full_ext[
            pop_index,
            1 - step_axial : 1 - step_axial + cells_axial,
            1 - step_cycle : 1 - step_cycle + cells_cycle,
        ]

    axial_pos = (lax.axis_index("coarse") * cells_axial + jnp.arange(cells_axial))[:, None, None]
    axial_total = cells_axial * lax.axis_size("coarse")
    radial_pos = jnp.arange(cells_radial)[None, None, :]
    results = []
    for pop_index in range(19):
        step_axial, step_cycle, step_radial = VELOCITIES[pop_index]
        shifted = source(pop_index)
        if step_radial == 1:
            shifted = jnp.concatenate(
                [jnp.zeros_like(shifted[:, :, :1]), shifted[:, :, :-1]], axis=2
            )
        elif step_radial == -1:
            shifted = jnp.concatenate(
                [shifted[:, :, 1:], jnp.zeros_like(shifted[:, :, :1])], axis=2
            )
        reflected = relaxed[opposite(pop_index)]
        if step_radial == 1:
            shifted = jnp.where(radial_pos == 0, reflected, shifted)
        elif step_radial == -1:
            shifted = jnp.where(
                radial_pos == cells_radial - 1, ghost_pops[pop_index][:, :, None], shifted
            )
        if step_axial == 1:
            shifted = jnp.where(axial_pos == 0, reflected, shifted)
        elif step_axial == -1:
            shifted = jnp.where(axial_pos == axial_total - 1, reflected, shifted)
        results.append(shifted)
    return jnp.stack(results)


def local(
    fine_populations,
    coarse_face,
    ghost_map,
    marker_force,
    marker_weights,
    marker_tiles,
    block_counts,
):
    cells_axial, cells_cycle, cells_radial = fine_populations.shape[1:]
    force_field = spread_markers(
        marker_force,
        marker_weights,
        marker_tiles,
        block_counts,
        cells_axial,
        cells_cycle,
        cells_radial,
    )
    face_index = ghost_map.reshape(-1)
    following = passed_along(coarse_face, "sector", -1)
    window = jnp.concatenate([coarse_face, following], axis=2)
    current = fine_populations
    for substep in range(2):
        weight_new = 0.5 * (substep + 1)
        blended = (1.0 - weight_new) * window[0] + weight_new * window[1]
        ghost_pops = interface_values(blended[:, face_index].reshape(19, cells_axial, cells_cycle))
        relaxed = collide(current, force_field)
        current = stream(relaxed, ghost_pops)
    return current


def solution(mesh):
    in_specs = (
        P(None, "coarse", "sector", None),
        P(None, None, ("coarse", "sector")),
        P("coarse", "sector"),
        P(("coarse", "sector"), None, None),
        P(("coarse", "sector"), None, None),
        P(("coarse", "sector")),
        P(("coarse", "sector")),
    )
    out_specs = P(None, "coarse", "sector", None)
    return jax.shard_map(local, mesh=mesh, in_specs=in_specs, out_specs=out_specs, check_vma=False)
```

profile of v0, /device:TPU:1, one launch (start us, length us, event | category | flops | bytes accessed | tf_op | source)
XLA Modules:
  0.0 129.4 jit_solution(6774819186579456769)
XLA Ops:
  0.0 9.4 %collective-permute-start.6 = (f32[2,19,128]{2,0,1:T(2,128)}, f32[2,19,128]{2,0,1:T(2,128)S(1)}, u32[]{:S(2)}, u32[]{:S(2)}) collective-permute-start(f32[2,19,128]{2,0,1:T(2,128)} %param.12), channel_id=1, source_target_pairs={{0,31},{1,0},{2,1},{3,2},{4,3},{5,4},{6,5},{7,6},{8,7},{9,8},{10,9... | collective-permute-start | bytes 58376 | tf_op jit(solution)/shard_map/ppermute | solution.py:54
  10.1 0.7 compare_select_fusion.1
  10.7 1.1 convolution_select_fusion
  12.0 1.6 %scatter_fusion = f32[3,576,128]{2,0,1:T(4,128)S(1)} fusion(f32[3,576,128]{2,0,1:T(4,128)S(1)} %broadcast_in_dim.251, s32[32]{0:T(128)S(1)} %compare_select_fusion.1, f32[32,3,128]{2,1,0:T(4,128)S(1)} %convolution_select_fusion), kind=kCustom, calls=%fused_computation.2 | custom fusion | flops 12288 | bytes 147584 | tf_op jit(solution)/shard_map/scatter-add | solution.py:137
  13.9 7.2 %collective-permute-start.1 = (f32[3,32,1,128]{3,2,1,0:T(1,128)S(1)}, f32[3,32,1,128]{3,2,1,0:T(1,128)}, u32[]{:S(2)}, u32[]{:S(2)}) collective-permute-start(f32[3,32,1,128]{3,2,1,0:T(1,128)S(1)} %copy.34), channel_id=1, source_target_pairs={{1,0},{2,1},{3,2},{4,3},{5,4},{6,5},{7,6},{8,7},{9,8},{10,9},{11,1... | collective-permute-start | bytes 147464 | tf_op jit(solution)/shard_map/ppermute | solution.py:44
  21.2 0.7 constant_dynamic-update-slice_fusion.1
  21.9 0.8 copy.30
  23.5 1.0 gather_fusion
  24.5 2.6 %slice_reduce_fusion.36 = (f32[512]{0:T(512)S(1)}, f32[512]{0:T(512)S(1)}, f32[512]{0:T(512)S(1)}, f32[512]{0:T(512)S(1)}, f32[512]{0:T(512)S(1)}, /*index=5*/f3...) fusion(f32[19,512]{0,1:T(8,128)S(1)} %bitcast.739), kind=kLoop, calls=%fused_computation.540 | loop fusion | bytes 77824 | tf_op jit(solution)/shard_map/slice | solution.py:77
  28.8 1.2 gather_fusion.1
  30.0 0.9 copy_add_fusion
  30.9 2.6 %scatter-add.18 = f32[3,32,16,128]{3,2,1,0:T(8,128)S(1)} dynamic-update-slice(f32[3,32,16,128]{3,2,1,0:T(8,128)S(1)} %copy.31, f32[3,32,1,128]{3,2,1,0:T(1,128)S(1)} %copy_add_fusion, s32[]{:T(128)} %constant.136.clone.1, s32[]{:T(128)} %constant.136.clone.1, s32[]{:T(128)} %constant.136.clone.1, s32[]{:T(128)} %constant.136.clone.1) | dynamic-update-slice | bytes 98308 | tf_op jit(solution)/shard_map/scatter-add | solution.py:142
  33.5 0.9 slice_add_fusion
  34.3 2.6 %scatter-add.19 = f32[3,32,16,128]{3,2,1,0:T(8,128)S(1)} dynamic-update-slice(f32[3,32,16,128]{3,2,1,0:T(8,128)S(1)} %scatter-add.18, f32[3,32,1,128]{3,2,1,0:T(1,128)S(1)} %slice_add_fusion, s32[]{:T(128)} %constant.136.clone.1, s32[]{:T(128)} %constant.136.clone.1, s32[]{:T(128)} %constant.138.clone.1, s32[]{:T(128)} %constant.136.clone.1) | dynamic-update-slice | bytes 98308 | tf_op jit(solution)/shard_map/scatter-add | solution.py:143
  36.9 3.2 %add_dynamic-update-slice_fusion = (f32[19,32,16,128]{3,2,1,0:T(8,128)S(1)}, f32[1,32,16,128]{3,2,1,0:T(8,128)S(1)}, f32[1,32,16,128]{3,2,1,0:T(8,128)S(1)}, f32...) fusion(f32[19,32,16,128]{3,2,1,0:T(8,128)} %param.11, ...), kind=kLoop, calls=%fused_computation.682 | loop fusion | flops 4849663 | bytes 7602176
  40.1 0.5 slice-done.1
  44.0 0.7 fusion.507
  44.7 1.4 %collective-permute-start.2 = (f32[19,32,1,128]{3,2,1,0:T(1,128)S(1)}, f32[19,32,1,128]{3,2,1,0:T(1,128)S(1)}, u32[]{:S(2)}, u32[]{:S(2)}) collective-permute-start(f32[19,32,1,128]{3,2,1,0:T(1,128)S(1)} %get-tuple-element.173), channel_id=1, source_target_pairs={{0,1},{1,2},{2,3},{3,4},{4,5},{5,6},{6,7},{7,8},{8,9},{9,10},{10,1... | collective-permute-start | bytes 933896 | tf_op jit(solution)/shard_map/ppermute | solution.py:42
  46.2 0.7 fusion.439
  47.1 5.0 %collective-permute-done.3 = f32[19,32,1,128]{3,2,1,0:T(1,128)S(1)} collective-permute-done((f32[19,32,1,128]{3,2,1,0:T(1,128)S(1)}, f32[19,32,1,128]{3,2,1,0:T(1,128)S(1)}, u32[]{:S(2)}, u32[]{:S(2)}) %collective-permute-start.3) | collective-permute-done | bytes 311328 | tf_op jit(solution)/shard_map/ppermute | solution.py:44
  52.0 5.8 %collective-permute-done.2 = f32[19,32,1,128]{3,2,1,0:T(1,128)S(1)} collective-permute-done((f32[19,32,1,128]{3,2,1,0:T(1,128)S(1)}, f32[19,32,1,128]{3,2,1,0:T(1,128)S(1)}, u32[]{:S(2)}, u32[]{:S(2)}) %collective-permute-start.2) | collective-permute-done | bytes 311328 | tf_op jit(solution)/shard_map/ppermute | solution.py:42
  57.9 4.5 %collective-permute-start.5 = (f32[19,1,18,128]{3,2,1,0:T(8,128)S(1)}, f32[19,1,18,128]{3,2,1,0:T(8,128)S(1)}, u32[]{:S(2)}, u32[]{:S(2)}) collective-permute-start(f32[19,1,18,128]{3,2,1,0:T(8,128)S(1)} %get-tuple-element.155), channel_id=1, source_target_pairs={{32,0},{64,32},{96,64},{33,1},{65,33},{97,65},{34,2},{66,34},{98,6... | collective-permute-start | bytes 525320 | tf_op jit(solution)/shard_map/ppermute | solution.py:44
  62.4 2.4 %collective-permute-start.4 = (f32[19,1,18,128]{3,2,1,0:T(8,128)S(1)}, f32[19,1,18,128]{3,2,1,0:T(8,128)S(1)}, u32[]{:S(2)}, u32[]{:S(2)}) collective-permute-start(f32[19,1,18,128]{3,2,1,0:T(8,128)S(1)} %get-tuple-element.156), channel_id=1, source_target_pairs={{0,32},{32,64},{64,96},{1,33},{33,65},{65,97},{2,34},{34,66},{66,9... | collective-permute-start | bytes 525320 | tf_op jit(solution)/shard_map/ppermute | solution.py:42
  65.4 0.9 collective-permute-done.5
  66.4 1.2 collective-permute-done.4
  68.0 4.5 %multiply_add_fusion = (f32[32,16,128]{2,1,0:T(8,128)S(1)}, f32[32,16,128]{2,1,0:T(8,128)S(1)}, f32[32,16,128]{2,1,0:T(8,128)S(1)}, f32[32,16,128]{2,1,0:T(8,128...) fusion(f32[32,16,128]{2,1,0:T(8,128)S(1)} %get-tuple-element.12, ...), kind=kLoop, calls=%fused_computation.672 | loop fusion | flops 22544384 | bytes 20361536 | tf_op jit(solution)/shard_map/add | solution.py:108
  72.5 2.3 %copy.80 = f32[19,32,16,128]{3,2,1,0:T(8,128)} copy(f32[19,32,16,128]{3,2,1,0:T(8,128)S(1)} %bitcast_dynamic-update-slice_fusion.22) | data formatting | bytes 9961472
  74.7 0.9 bitcast_dynamic-update-slice_fusion.21
  75.6 0.9 bitcast_dynamic-update-slice_fusion.20
  76.8 0.8 bitcast_dynamic-update-slice_fusion.19
  78.7 0.9 bitcast_dynamic-update-slice_fusion.13
  79.5 0.9 bitcast_dynamic-update-slice_fusion.12
  80.4 0.9 bitcast_dynamic-update-slice_fusion.11
  81.3 0.9 bitcast_dynamic-update-slice_fusion.10
  82.4 0.9 bitcast_dynamic-update-slice_fusion.9
  83.3 0.9 bitcast_dynamic-update-slice_fusion.8
  84.4 2.2 %copy-done.1 = f32[19,32,16,128]{3,2,1,0:T(8,128)} copy-done((f32[19,32,16,128]{3,2,1,0:T(8,128)}, f32[19,32,16,128]{3,2,1,0:T(8,128)S(1)}, u32[]{:S(2)}) %copy-start.1) | copy-done | bytes 4980760
  86.6 1.5 %fusion.506 = (f32[19,32,1,128]{3,2,1,0:T(1,128)}, f32[19,32,1,128]{3,2,1,0:T(1,128)}) fusion(f32[19,32,16,128]{3,2,1,0:T(8,128)S(1)} %fusion.379), kind=kLoop, calls=%fused_computation.783 | loop fusion | bytes 1245184 | tf_op jit(solution)/shard_map/slice | solution.py:39
  88.1 7.2 %collective-permute-start.8 = (f32[19,32,1,128]{3,2,1,0:T(1,128)}, f32[19,32,1,128]{3,2,1,0:T(1,128)S(1)}, u32[]{:S(2)}, u32[]{:S(2)}) collective-permute-start(f32[19,32,1,128]{3,2,1,0:T(1,128)} %get-tuple-element.167), channel_id=1, source_target_pairs={{1,0},{2,1},{3,2},{4,3},{5,4},{6,5},{7,6},{8,7},{9,8},{10,9},{11,1... | collective-permute-start | bytes 933896 | tf_op jit(solution)/shard_map/ppermute | solution.py:44
  95.3 2.6 %slice_reduce_fusion.17 = (f32[512]{0:T(512)S(1)}, f32[512]{0:T(512)S(1)}, f32[512]{0:T(512)S(1)}, f32[512]{0:T(512)S(1)}, f32[512]{0:T(512)S(1)}, /*index=5*/f3...) fusion(f32[19,512]{0,1:T(8,128)S(1)} %bitcast.738), kind=kLoop, calls=%fused_computation.491 | loop fusion | bytes 77824 | tf_op jit(solution)/shard_map/slice | solution.py:77
  99.5 2.5 %collective-permute-done.7 = f32[19,32,1,128]{3,2,1,0:T(1,128)S(1)} collective-permute-done((f32[19,32,1,128]{3,2,1,0:T(1,128)}, f32[19,32,1,128]{3,2,1,0:T(1,128)S(1)}, u32[]{:S(2)}, u32[]{:S(2)}) %collective-permute-start.7) | collective-permute-done | bytes 311328 | tf_op jit(solution)/shard_map/ppermute | solution.py:42
  102.0 1.1 pad_maximum_fusion.16
  103.1 4.0 %collective-permute-start.9 = (f32[19,1,18,128]{3,2,1,0:T(8,128)S(1)}, f32[19,1,18,128]{3,2,1,0:T(8,128)S(1)}, u32[]{:S(2)}, u32[]{:S(2)}) collective-permute-start(f32[19,1,18,128]{3,2,1,0:T(8,128)S(1)} %get-tuple-element.152), channel_id=1, source_target_pairs={{0,32},{32,64},{64,96},{1,33},{33,65},{65,97},{2,34},{34,66},{66,9... | collective-permute-start | bytes 525320 | tf_op jit(solution)/shard_map/ppermute | solution.py:42
  107.2 1.9 %collective-permute-start.10 = (f32[19,1,18,128]{3,2,1,0:T(8,128)S(1)}, f32[19,1,18,128]{3,2,1,0:T(8,128)S(1)}, u32[]{:S(2)}, u32[]{:S(2)}) collective-permute-start(f32[19,1,18,128]{3,2,1,0:T(8,128)S(1)} %get-tuple-element.151), channel_id=1, source_target_pairs={{32,0},{64,32},{96,64},{33,1},{65,33},{97,65},{34,2},{66,34},{98,6... | collective-permute-start | bytes 525320 | tf_op jit(solution)/shard_map/ppermute | solution.py:44
  109.2 0.9 collective-permute-done.9
  110.1 1.8 %fusion.405 = f32[19,32,16,128]{3,2,1,0:T(8,128)} fusion(f32[19,32,16,128]{3,2,1,0:T(8,128)} %copy.80, f32[32,16,128]{2,1,0:T(8,128)} %get-tuple-element.97, f32[19,1,18,128]{3,2,1,0:T(8,128)S(1)} %collective-permute-done.9, f32[19,32,1,128]{3,2,1,0:T(1,128)S(1)} %collective-permute-done.8, f32[19,32,16,128]{3,2,1,0:T(8,128)S(1)} %copy-done.2, ...), kind=kLoop, calls=%fused_computation.502 | loop fusion | flops 262144 | bytes 6302752
  111.8 2.8 %collective-permute-done.10 = f32[19,1,18,128]{3,2,1,0:T(8,128)S(1)} collective-permute-done((f32[19,1,18,128]{3,2,1,0:T(8,128)S(1)}, f32[19,1,18,128]{3,2,1,0:T(8,128)S(1)}, u32[]{:S(2)}, u32[]{:S(2)}) %collective-permute-start.10) | collective-permute-done | bytes 175136 | tf_op jit(solution)/shard_map/ppermute | solution.py:44
  114.6 0.8 fusion.402
  115.4 0.7 maximum_dynamic-update-slice_fusion.1
  116.2 0.7 maximum_dynamic-update-slice_fusion
  116.9 0.8 bitcast_dynamic-update-slice_fusion.7
  117.8 0.8 bitcast_dynamic-update-slice_fusion.6
  118.6 0.8 fusion.399
  119.4 0.9 fusion.384
  120.6 0.8 fusion.387
  121.6 0.8 fusion.386
  122.6 0.9 fusion.381
  123.4 0.9 bitcast_dynamic-update-slice_fusion.5
  124.3 0.9 bitcast_dynamic-update-slice_fusion.4
  125.2 0.9 fusion.383
  126.1 0.8 bitcast_dynamic-update-slice_fusion.3
  126.9 0.8 bitcast_dynamic-update-slice_fusion.2
  127.7 0.8 bitcast_dynamic-update-slice_fusion.1
  128.6 0.8 bitcast_dynamic-update-slice_fusion
  (137 shorter events, 11.4 us)
Async XLA Ops:
  0.0 10.7 %copy-start = (bf16[32,128,128]{2,1,0:T(8,128)(2,1)S(1)}, bf16[32,128,128]{2,1,0:T(8,128)(2,1)}, u32[]{:S(2)}) copy-start(bf16[32,128,128]{2,1,0:T(8,128)(2,1)} %param.15) | copy-start | bytes 3145732
  0.0 23.2 %collective-permute-start.6 = (f32[2,19,128]{2,0,1:T(2,128)}, f32[2,19,128]{2,0,1:T(2,128)S(1)}, u32[]{:S(2)}, u32[]{:S(2)}) collective-permute-start(f32[2,19,128]{2,0,1:T(2,128)} %param.12), channel_id=1, source_target_pairs={{0,31},{1,0},{2,1},{3,2},{4,3},{5,4},{6,5},{7,6},{8,7},{9,8},{10,9... | collective-permute-start | bytes 58376 | tf_op jit(solution)/shard_map/ppermute | solution.py:54
  13.8 16.2 %collective-permute-start = (f32[3,32,1,128]{3,2,1,0:T(1,128)S(1)}, f32[3,32,1,128]{3,2,1,0:T(1,128)}, u32[]{:S(2)}, u32[]{:S(2)}) collective-permute-start(f32[3,32,1,128]{3,2,1,0:T(1,128)S(1)} %copy.33), channel_id=1, source_target_pairs={{0,1},{1,2},{2,3},{3,4},{4,5},{5,6},{6,7},{7,8},{8,9},{9,10},{10,1... | collective-permute-start | bytes 147464 | tf_op jit(solution)/shard_map/ppermute | solution.py:42
  13.9 19.5 %collective-permute-start.1 = (f32[3,32,1,128]{3,2,1,0:T(1,128)S(1)}, f32[3,32,1,128]{3,2,1,0:T(1,128)}, u32[]{:S(2)}, u32[]{:S(2)}) collective-permute-start(f32[3,32,1,128]{3,2,1,0:T(1,128)S(1)} %copy.34), channel_id=1, source_target_pairs={{1,0},{2,1},{3,2},{4,3},{5,4},{6,5},{7,6},{8,7},{9,8},{10,9},{11,1... | collective-permute-start | bytes 147464 | tf_op jit(solution)/shard_map/ppermute | solution.py:44
  22.8 4.4 %copy-start.11 = (s32[1024]{0:T(1024)}, s32[1024]{0:T(1024)S(1)}, u32[]{:S(2)}) copy-start(s32[1024]{0:T(1024)S(1)} %pad_clamp_fusion) | copy-start | bytes 12292
  27.2 12.9 %slice-start = ((s8[4980736]{0:T(1024)(128)(4,1)}), s8[786432]{0:T(1024)(128)(4,1)S(1)}, s32[]{:S(2)}) async-start(s8[4980736]{0:T(1024)(128)(4,1)} %bitcast.740), calls=%async_computation | async-start | bytes 1572864
  36.9 3.7 %slice-start.1 = ((s8[4980736]{0:T(1024)(128)(4,1)}), s8[4194304]{0:T(1024)(128)(4,1)S(1)}, s32[]{:S(2)}) async-start(s8[4980736]{0:T(1024)(128)(4,1)} %bitcast.740), calls=%async_computation.1 | async-start | bytes 8388608
  44.6 7.4 %collective-permute-start.3 = (f32[19,32,1,128]{3,2,1,0:T(1,128)S(1)}, f32[19,32,1,128]{3,2,1,0:T(1,128)S(1)}, u32[]{:S(2)}, u32[]{:S(2)}) collective-permute-start(f32[19,32,1,128]{3,2,1,0:T(1,128)S(1)} %get-tuple-element.172), channel_id=1, source_target_pairs={{1,0},{2,1},{3,2},{4,3},{5,4},{6,5},{7,6},{8,7},{9,8},{10,9},{11,1... | collective-permute-start | bytes 933896 | tf_op jit(solution)/shard_map/ppermute | solution.py:44
  44.7 13.1 %collective-permute-start.2 = (f32[19,32,1,128]{3,2,1,0:T(1,128)S(1)}, f32[19,32,1,128]{3,2,1,0:T(1,128)S(1)}, u32[]{:S(2)}, u32[]{:S(2)}) collective-permute-start(f32[19,32,1,128]{3,2,1,0:T(1,128)S(1)} %get-tuple-element.173), channel_id=1, source_target_pairs={{0,1},{1,2},{2,3},{3,4},{4,5},{5,6},{6,7},{7,8},{8,9},{9,10},{10,1... | collective-permute-start | bytes 933896 | tf_op jit(solution)/shard_map/ppermute | solution.py:42
  57.9 8.5 %collective-permute-start.5 = (f32[19,1,18,128]{3,2,1,0:T(8,128)S(1)}, f32[19,1,18,128]{3,2,1,0:T(8,128)S(1)}, u32[]{:S(2)}, u32[]{:S(2)}) collective-permute-start(f32[19,1,18,128]{3,2,1,0:T(8,128)S(1)} %get-tuple-element.155), channel_id=1, source_target_pairs={{32,0},{64,32},{96,64},{33,1},{65,33},{97,65},{34,2},{66,34},{98,6... | collective-permute-start | bytes 525320 | tf_op jit(solution)/shard_map/ppermute | solution.py:44
  62.4 5.2 %collective-permute-start.4 = (f32[19,1,18,128]{3,2,1,0:T(8,128)S(1)}, f32[19,1,18,128]{3,2,1,0:T(8,128)S(1)}, u32[]{:S(2)}, u32[]{:S(2)}) collective-permute-start(f32[19,1,18,128]{3,2,1,0:T(8,128)S(1)} %get-tuple-element.156), channel_id=1, source_target_pairs={{0,32},{32,64},{64,96},{1,33},{33,65},{65,97},{2,34},{34,66},{66,9... | collective-permute-start | bytes 525320 | tf_op jit(solution)/shard_map/ppermute | solution.py:42
  84.4 2.2 %copy-start.1 = (f32[19,32,16,128]{3,2,1,0:T(8,128)}, f32[19,32,16,128]{3,2,1,0:T(8,128)S(1)}, u32[]{:S(2)}) copy-start(f32[19,32,16,128]{3,2,1,0:T(8,128)S(1)} %fusion.379) | copy-start | bytes 14942212
  88.1 13.9 %collective-permute-start.7 = (f32[19,32,1,128]{3,2,1,0:T(1,128)}, f32[19,32,1,128]{3,2,1,0:T(1,128)S(1)}, u32[]{:S(2)}, u32[]{:S(2)}) collective-permute-start(f32[19,32,1,128]{3,2,1,0:T(1,128)} %get-tuple-element.166), channel_id=1, source_target_pairs={{0,1},{1,2},{2,3},{3,4},{4,5},{5,6},{6,7},{7,8},{8,9},{9,10},{10,1... | collective-permute-start | bytes 933896 | tf_op jit(solution)/shard_map/ppermute | solution.py:42
  88.1 13.9 %collective-permute-start.8 = (f32[19,32,1,128]{3,2,1,0:T(1,128)}, f32[19,32,1,128]{3,2,1,0:T(1,128)S(1)}, u32[]{:S(2)}, u32[]{:S(2)}) collective-permute-start(f32[19,32,1,128]{3,2,1,0:T(1,128)} %get-tuple-element.167), channel_id=1, source_target_pairs={{1,0},{2,1},{3,2},{4,3},{5,4},{6,5},{7,6},{8,7},{9,8},{10,9},{11,1... | collective-permute-start | bytes 933896 | tf_op jit(solution)/shard_map/ppermute | solution.py:44
  99.4 10.6 %copy-start.2 = (f32[19,32,16,128]{3,2,1,0:T(8,128)S(1)}, f32[19,32,16,128]{3,2,1,0:T(8,128)}, u32[]{:S(2)}) copy-start(f32[19,32,16,128]{3,2,1,0:T(8,128)} %copy-done.1) | copy-start | bytes 14942212
  103.1 11.5 %copy-start.9 = (f32[32,16,128]{2,1,0:T(8,128)S(1)}, f32[32,16,128]{2,1,0:T(8,128)}, u32[]{:S(2)}) copy-start(f32[32,16,128]{2,1,0:T(8,128)} %get-tuple-element.99) | copy-start | bytes 786436
  103.1 7.0 %collective-permute-start.9 = (f32[19,1,18,128]{3,2,1,0:T(8,128)S(1)}, f32[19,1,18,128]{3,2,1,0:T(8,128)S(1)}, u32[]{:S(2)}, u32[]{:S(2)}) collective-permute-start(f32[19,1,18,128]{3,2,1,0:T(8,128)S(1)} %get-tuple-element.152), channel_id=1, source_target_pairs={{0,32},{32,64},{64,96},{1,33},{33,65},{65,97},{2,34},{34,66},{66,9... | collective-permute-start | bytes 525320 | tf_op jit(solution)/shard_map/ppermute | solution.py:42
  107.2 7.4 %collective-permute-start.10 = (f32[19,1,18,128]{3,2,1,0:T(8,128)S(1)}, f32[19,1,18,128]{3,2,1,0:T(8,128)S(1)}, u32[]{:S(2)}, u32[]{:S(2)}) collective-permute-start(f32[19,1,18,128]{3,2,1,0:T(8,128)S(1)} %get-tuple-element.151), channel_id=1, source_target_pairs={{32,0},{64,32},{96,64},{33,1},{65,33},{97,65},{34,2},{66,34},{98,6... | collective-permute-start | bytes 525320 | tf_op jit(solution)/shard_map/ppermute | solution.py:44
  115.4 1.5 %copy-start.10 = (f32[32,16,128]{2,1,0:T(8,128)S(1)}, f32[32,16,128]{2,1,0:T(8,128)}, u32[]{:S(2)}) copy-start(f32[32,16,128]{2,1,0:T(8,128)} %get-tuple-element.95) | copy-start | bytes 786436
  121.4 1.1 copy-start.6
  121.4 2.0 %copy-start.4 = (f32[32,16,128]{2,1,0:T(8,128)S(1)}, f32[32,16,128]{2,1,0:T(8,128)}, u32[]{:S(2)}) copy-start(f32[32,16,128]{2,1,0:T(8,128)} %get-tuple-element.83) | copy-start | bytes 786436
  121.4 2.9 %copy-start.5 = (f32[32,16,128]{2,1,0:T(8,128)S(1)}, f32[32,16,128]{2,1,0:T(8,128)}, u32[]{:S(2)}) copy-start(f32[32,16,128]{2,1,0:T(8,128)} %get-tuple-element.77) | copy-start | bytes 786436
  121.5 3.6 %copy-start.3 = (f32[32,16,128]{2,1,0:T(8,128)S(1)}, f32[32,16,128]{2,1,0:T(8,128)}, u32[]{:S(2)}) copy-start(f32[32,16,128]{2,1,0:T(8,128)} %get-tuple-element.79) | copy-start | bytes 786436
  121.6 4.5 %copy-start.8 = (f32[32,16,128]{2,1,0:T(8,128)S(1)}, f32[32,16,128]{2,1,0:T(8,128)}, u32[]{:S(2)}) copy-start(f32[32,16,128]{2,1,0:T(8,128)} %get-tuple-element.75) | copy-start | bytes 786436
  121.6 7.0 %copy-start.7 = (f32[32,16,128]{2,1,0:T(8,128)S(1)}, f32[32,16,128]{2,1,0:T(8,128)}, u32[]{:S(2)}) copy-start(f32[32,16,128]{2,1,0:T(8,128)} %get-tuple-element.73) | copy-start | bytes 786436
where the time goes:
time: 130 us; the launch traced here: 129 us
  other arithmetic  43.3 us (33%)
  starting transfers between devices  38.2 us (29%)
  local copies, waits for them, and re-layouts  26.4 us (20%)
  waiting for transfers between devices  19.1 us (15%)
  between operations  1.35 us (1%)
    unnamed x49, other arithmetic  28.1 us
    ppermute x5, starting transfers between devices, extended(): lax.ppermute(head, axis, [((i + 1) % count, i) for i in range(ends)])  20.9 us
    ppermute x5, waiting for transfers between devices, extended(): lax.ppermute(tail, axis, [(i, (i + 1) % count) for i in range(ends)])  10.3 us
    ppermute x1, starting transfers between devices, passed_along(): return lax.ppermute(value, axis, pairs)  9.41 us
    ppermute x5, waiting for transfers between devices, extended(): lax.ppermute(head, axis, [((i + 1) % count, i) for i in range(ends)])  8.73 us
    ppermute x5, starting transfers between devices, extended(): lax.ppermute(tail, axis, [(i, (i + 1) % count) for i in range(ends)])  7.86 us
    unnamed x37, local copies, waits for them, and re-layouts  6.92 us
    add x3, other arithmetic, collide(): populations[pop_index] - (populations[pop_index] - balance) / TAU_FINE  5.26 us
  transfers between devices with their start and end apart: 11, of which 7 were waited for; matrix products, arithmetic and copies ran while one was open for 18% of the time, Pallas kernels for 0%

commit v1 on v0

v1 whole, which is shorter than its diff:
```python
import functools

import jax
import jax.numpy as jnp
from jax import lax
from jax.experimental import pallas as pl
from jax.experimental.pallas import tpu as pltpu
from jax.sharding import PartitionSpec as P

VELOCITIES = (
    (0, 0, 0),
    (1, 0, 0),
    (-1, 0, 0),
    (0, 1, 0),
    (0, -1, 0),
    (0, 0, 1),
    (0, 0, -1),
    (1, 1, 0),
    (-1, -1, 0),
    (1, -1, 0),
    (-1, 1, 0),
    (1, 0, 1),
    (-1, 0, -1),
    (1, 0, -1),
    (-1, 0, 1),
    (0, 1, 1),
    (0, -1, -1),
    (0, 1, -1),
    (0, -1, 1),
)
LATTICE_WEIGHTS = (1.0 / 3.0,) + (1.0 / 18.0,) * 6 + (1.0 / 36.0,) * 12
TAU_FINE = 0.8
TAU_COARSE = 0.65
FORCE_FACTOR = 1.0 - 0.5 / TAU_FINE
RESCALE = TAU_FINE / (2.0 * TAU_COARSE)

FA, FR, FW = 32, 16, 128
NB, MB = 32, 128
PLANE = 24
OFF = 32
ROWS = OFF + FA * PLANE + PLANE

UP = [i for i in range(19) if VELOCITIES[i][0] == 1]
DOWN = [i for i in range(19) if VELOCITIES[i][0] == -1]
FORTH = [i for i in range(19) if VELOCITIES[i][1] == 1]
BACK = [i for i in range(19) if VELOCITIES[i][1] == -1]
INWARD = [i for i in range(19) if VELOCITIES[i][2] == -1]
ORDER = UP + DOWN + [i for i in range(19) if VELOCITIES[i][0] == 0]
SLOT = {pop: slot for slot, pop in enumerate(ORDER)}

RIM_BACK, RIM_FORTH, GHOST = 0, 1, 2
EXCHANGE = 3
N_REMOTE = EXCHANGE + 16

MESH = pl.DeviceIdType.MESH


def opposite(pop_index):
    if pop_index == 0:
        return 0
    return pop_index + 1 if pop_index % 2 == 1 else pop_index - 1


def collide(f, force, scale):
    gain = -4.0 / scale
    s, d = {}, {}
    for i in range(1, 19, 2):
        s[i] = f[i] + f[i + 1]
        d[i] = f[i] - f[i + 1]
    density = ((f[0] + s[1]) + (s[3] + s[5])) + ((s[7] + s[9]) + (s[11] + s[13])) + (s[15] + s[17])
    momentum = [
        d[1] + (d[7] + d[9]) + (d[11] + d[13]),
        d[3] + (d[7] - d[9]) + (d[15] + d[17]),
        d[5] + (d[11] - d[13]) + (d[15] - d[17]),
    ]
    guess = pl.reciprocal(density, approx=True)
    inverse = guess * (2.0 - density * guess)
    pushed = [momentum[k] + (0.5 / scale) * force[k] for k in range(3)]
    u = [pushed[k] * inverse for k in range(3)]
    h = [(-22.5 / 36.0) * pushed[k] + (gain * 3.375 / 36.0) * force[k] for k in range(3)]
    q = [(-15.0 / 36.0) * pushed[k] + (gain * 1.125 / 36.0) * force[k] for k in range(3)]
    t = [u[k] * h[k] for k in range(3)]
    base = (-5.0 / 36.0) * density - (1.0 / 3.0) * (t[0] + t[1] + t[2])
    out = [None] * 19
    out[0] = f[0] + 12.0 * base
    for k, i in enumerate((1, 3, 5)):
        even = 2.0 * (base + t[k])
        odd = 2.0 * q[k]
        out[i] = f[i] + (even + odd)
        out[i + 1] = f[i + 1] + (even - odd)
    for a, b, i in ((0, 1, 7), (0, 2, 11), (1, 2, 15)):
        common = base + t[a] + t[b]
        cross = u[a] * h[b] + u[b] * h[a]
        for j, even, odd in (
            (i, common + cross, q[a] + q[b]),
            (i + 2, common - cross, q[a] - q[b]),
        ):
            out[j] = f[j] + (even + odd)
            out[j + 1] = f[j + 1] + (even - odd)
    return out


def interface_rows(pops):
    density = pops[0]
    for i in range(1, 19):
        density = density + pops[i]
    velocity = []
    for k in range(3):
        running = jnp.zeros_like(density)
        for i in range(19):
            if VELOCITIES[i][k] == 1:
                running = running + pops[i]
            elif VELOCITIES[i][k] == -1:
                running = running - pops[i]
        velocity.append(running / density)
    speed_sq = velocity[0] * velocity[0] + velocity[1] * velocity[1] + velocity[2] * velocity[2]
    rows = []
    for i in INWARD:
        dotted = jnp.zeros_like(density)
        for k in range(3):
            if VELOCITIES[i][k] == 1:
                dotted = dotted + velocity[k]
            elif VELOCITIES[i][k] == -1:
                dotted = dotted - velocity[k]
        weight = LATTICE_WEIGHTS[i]
        balance = weight * density * (1.0 + 3.0 * dotted + 4.5 * dotted * dotted - 1.5 * speed_sq)
        rows.append(balance + RESCALE * (pops[i] - balance))
    return rows


def pulled(load, ghost, first_column, low, high):
    lane = lax.broadcasted_iota(jnp.int32, (8, FW), 1)
    inner = lane == 0
    outer = lane == FW - 1
    values = []
    for i in range(19):
        ca, cr, cw = VELOCITIES[i]
        value = load(i, -ca, -cr)
        ended = low if ca == 1 else high if ca == -1 else None
        if cw == 1 or ended is not None:
            reflected = load(opposite(i), 0, 0)
        if cw == 1:
            value = jnp.where(inner, reflected, pltpu.roll(value, 1, 1))
        elif cw == -1:
            shift = FW - 1 - (first_column + INWARD.index(i))
            value = jnp.where(outer, pltpu.roll(ghost, shift, 1), pltpu.roll(value, FW - 1, 1))
        if ended is not None:
            value = jnp.where(ended, reflected, value)
        values.append(value)
    return values


def pull_plane(relaxed, ghosts, first_column, a, half, low, high):
    row = OFF + a * PLANE + half * 8

    def load(i, da, dr):
        return relaxed[SLOT[i], pl.ds(row + da * PLANE + dr, 8), :]

    ghost = ghosts[pl.ds(a * FR + half * 8, 8), :]
    return pulled(load, ghost, first_column, low, high)


def pull_rim(relaxed, margin_back, margin_forth, ghosts, first_column, c, r, first, last):
    row = OFF + c * (8 * PLANE) + r

    def load(i, da, dr):
        if r + dr < 0:
            return margin_back[FORTH.index(i), pl.ds(8 + c * 8 + da, 8), :]
        if r + dr >= FR:
            return margin_forth[BACK.index(i), pl.ds(8 + c * 8 + da, 8), :]
        return relaxed[SLOT[i], pl.ds(row + da * PLANE + dr, 8, stride=PLANE), :]

    ghost = ghosts[pl.ds(c * (8 * FR) + r, 8, stride=FR), :]
    along = lax.broadcasted_iota(jnp.int32, (8, FW), 0) + c * 8
    low = along == jnp.where(first, 0, -1)
    high = along == jnp.where(last, FA - 1, -1)
    return pulled(load, ghost, first_column, low, high)


def end_mask(flag):
    return lax.broadcasted_iota(jnp.int32, (8, FW), 0) < jnp.where(flag, 8, 0)


def split(x):
    high = x.astype(jnp.bfloat16)
    rest = x - high.astype(jnp.float32)
    middle = rest.astype(jnp.bfloat16)
    low = (rest - middle.astype(jnp.float32)).astype(jnp.bfloat16)
    return high, middle, low


def advance(
    n_coarse,
    n_sector,
    fine_hbm,
    face_hbm,
    map_hbm,
    mforce_hbm,
    mweights_hbm,
    tiles_hbm,
    count_ref,
    relaxed2,
    back2,
    forth2,
    ghosts,
    fine,
    face,
    gmap,
    mforce,
    mweights,
    tiles_ref,
    rows3,
    parts,
    force,
    rim_back,
    rim_forth,
    gown,
    gnext,
    relaxed1,
    back1,
    forth1,
    sends,
    local_sem,
    send_sem,
    recv_sem,
):
    p = lax.axis_index("coarse")
    s = lax.axis_index("sector")
    ahead = lax.rem(s + 1, n_sector)
    behind = lax.rem(s + n_sector - 1, n_sector)
    first, last = p == 0, p == n_coarse - 1
    has_low, has_high = p > 0, p < n_coarse - 1

    loads = [
        pltpu.make_async_copy(mweights_hbm, mweights, local_sem.at[0]),
        pltpu.make_async_copy(mforce_hbm, mforce, local_sem.at[1]),
        pltpu.make_async_copy(face_hbm, face, local_sem.at[2]),
        pltpu.make_async_copy(map_hbm, gmap, local_sem.at[3]),
        pltpu.make_async_copy(tiles_hbm, tiles_ref, local_sem.at[8]),
    ]
    for c in range(4):
        rows = pl.ds(c * 128, 128)
        loads.append(
            pltpu.make_async_copy(fine_hbm.at[:, rows, :], fine.at[:, rows, :], local_sem.at[4 + c])
        )
    for copy in loads:
        copy.start()

    barrier = pltpu.get_barrier_semaphore()

    def greet(coarse, sector):
        pl.semaphore_signal(
            barrier, inc=1, device_id={"coarse": coarse, "sector": sector}, device_id_type=MESH
        )

    greet(p, ahead)
    greet(p, behind)
    for there, coarse in ((has_low, p - 1), (has_high, p + 1)):

        @pl.when(there)
        def _():
            greet(coarse, s)
            greet(coarse, ahead)
            greet(coarse, behind)

    loads[1].wait()
    for k in range(3):
        rows3[pl.ds(k, NB, stride=8), :] = mforce[k].astype(jnp.float32)
    loads[0].wait()

    def block(b, carry):
        for k in range(4):
            n = b * 4 + k
            rows = pl.ds(pl.multiple_of(n * 8, 8), 8)
            parts[rows, :] = jnp.dot(
                rows3[rows, :].astype(jnp.bfloat16),
                mweights[n],
                preferred_element_type=jnp.float32,
            )
        return carry

    lax.fori_loop(0, NB // 4, block, 0)
    loads[4].wait()
    block_id = lax.rem(lax.broadcasted_iota(jnp.int32, (8, 3 * NB), 1), NB)
    tile = jnp.zeros((8, 3 * NB), jnp.int32)
    for b in range(NB):
        tile = jnp.where(block_id == b, tiles_ref[b], tile)
    axial = lax.shift_right_logical(tile * 3641, 16)
    cycle = tile - axial * (FR + 2)
    target = jnp.where(
        cycle == 0,
        FA * FR + axial,
        jnp.where(cycle == FR + 1, FA * FR + FA + axial, axial * FR + cycle - 1),
    )
    target = jnp.where(block_id < count_ref[0], target, -1)[:1]
    columns = []
    for k in range(3):
        high, middle, low = split(parts[pl.ds(k, NB, stride=8), :])
        columns.append(jnp.concatenate([high, middle, low], axis=0))
    columns = jnp.concatenate(columns, axis=1)
    for n in range(9):
        cell = lax.broadcasted_iota(jnp.int32, (64, 3 * NB), 0) + n * 64
        chosen = jnp.where(cell == target, 1.0, 0.0).astype(jnp.bfloat16)
        summed = jnp.dot(chosen, columns, preferred_element_type=jnp.float32)
        for k in range(3):
            force[k, n * 64 : n * 64 + 64, :] = summed[:, k * FW : k * FW + FW]

    peers = 2 + jnp.where(has_low, 3, 0) + jnp.where(has_high, 3, 0)
    pl.semaphore_wait(barrier, peers)

    def send(n, src, dst, coarse, sector):
        return pltpu.make_async_remote_copy(
            src_ref=src,
            dst_ref=dst,
            send_sem=send_sem.at[n],
            recv_sem=recv_sem.at[n],
            device_id={"coarse": coarse, "sector": sector},
            device_id_type=MESH,
        )

    rims = [
        send(RIM_BACK, force.at[:, 512:544, :], rim_forth, p, behind),
        send(RIM_FORTH, force.at[:, 544:576, :], rim_back, p, ahead),
    ]
    for copy in rims:
        copy.start()

    loads[2].wait()
    for k in range(2):
        new = 0.5 * (k + 1)
        pops = [
            (1.0 - new) * face[i, 0:1, :] + new * face[i, 1:2, :] for i in range(19)
        ]
        for j, row in enumerate(interface_rows(pops)):
            gown[5 * k + j : 5 * k + j + 1, :] = row * (-4.0, 16.0)[k]
    for j in range(10, 16):
        gown[j : j + 1, :] = jnp.zeros((1, FW), jnp.float32)
    ghost_copy = send(GHOST, gown, gnext, p, behind)
    ghost_copy.start()

    def exchange(k, relaxed, back, forth):
        base = EXCHANGE + 8 * k
        top, bottom = OFF + (FA - 1) * PLANE, OFF
        to_back, to_forth = sends.at[2 * k], sends.at[2 * k + 1]
        both = [
            send(base, to_forth, back.at[:, 8:40, :], p, ahead),
            send(base + 1, to_back, forth.at[:, 8:40, :], p, behind),
        ]
        up7, down10 = FORTH.index(7), FORTH.index(10)
        up9, down8 = BACK.index(9), BACK.index(8)
        upward = [
            send(
                base + 2,
                relaxed.at[0:5, top : top + FR, :],
                relaxed.at[0:5, bottom - PLANE : bottom - PLANE + FR, :],
                p + 1,
                s,
            ),
            send(base + 3, to_forth.at[up7, 24:32, :], back.at[up7, 0:8, :], p + 1, ahead),
            send(base + 4, to_back.at[up9, 24:32, :], forth.at[up9, 0:8, :], p + 1, behind),
        ]
        downward = [
            send(
                base + 5,
                relaxed.at[5:10, bottom : bottom + FR, :],
                relaxed.at[5:10, top + PLANE : top + PLANE + FR, :],
                p - 1,
                s,
            ),
            send(base + 6, to_forth.at[down10, 0:8, :], back.at[down10, 40:48, :], p - 1, ahead),
            send(base + 7, to_back.at[down8, 0:8, :], forth.at[down8, 40:48, :], p - 1, behind),
        ]
        return both, upward, downward

    def start(copies):
        both, upward, downward = copies
        for copy in both:
            copy.start()
        for there, group in ((has_high, upward), (has_low, downward)):

            @pl.when(there)
            def _():
                for copy in group:
                    copy.start()

    def arrive(copies):
        both, upward, downward = copies
        for copy in both:
            copy.wait_recv()
        for there, group in ((has_low, upward), (has_high, downward)):

            @pl.when(there)
            def _():
                for copy in group:
                    copy.wait_recv()

    def leave(copies):
        both, upward, downward = copies
        for copy in both:
            copy.wait_send()
        for there, group in ((has_high, upward), (has_low, downward)):

            @pl.when(there)
            def _():
                for copy in group:
                    copy.wait_send()

    def keep_plane(relaxed, a, half, values):
        row = pl.multiple_of(OFF + a * PLANE + half * 8, 8)
        for i in range(19):
            relaxed[SLOT[i], pl.ds(row, 8), :] = values[i]

    def keep_rim(k, relaxed, c, r, values):
        row = OFF + c * (8 * PLANE) + r
        for i in range(19):
            relaxed[SLOT[i], pl.ds(row, 8, stride=PLANE), :] = values[i]
        for j, i in enumerate(BACK if r == 0 else FORTH):
            side = 2 * k if r == 0 else 2 * k + 1
            sends[side, j, pl.ds(pl.multiple_of(c * 8, 8), 8), :] = values[i]

    def plane1(a, carry):
        for half in range(2):
            row = pl.multiple_of(a * FR + half * 8, 8)
            f = [fine[i, pl.ds(row, 8), :] for i in range(19)]
            push = [force[k, pl.ds(row, 8), :] for k in range(3)]
            keep_plane(relaxed1, a, half, collide(f, push, 1.0))
        return carry

    def rim1(c, carry):
        for r, rim in ((0, rim_back), (FR - 1, rim_forth)):
            rows = pl.ds(c * (8 * FR) + r, 8, stride=FR)
            f = [fine[i, rows, :] for i in range(19)]
            along = pl.ds(pl.multiple_of(c * 8, 8), 8)
            push = [force[k, rows, :] + rim[k, along, :] for k in range(3)]
            for k in range(3):
                force[k, rows, :] = push[k]
            keep_rim(0, relaxed1, c, r, collide(f, push, 1.0))
        return carry

    for c in range(4):
        loads[5 + c].wait()
        lax.fori_loop(c * 8, c * 8 + 8, plane1, 0)
    for copy in rims:
        copy.wait_recv()
    lax.fori_loop(0, 4, rim1, 0)
    copies1 = exchange(0, relaxed1, back1, forth1)
    start(copies1)

    loads[3].wait()
    ghost_copy.wait_recv()
    window = jnp.concatenate([gown[...], gnext[...]], axis=1)
    turned = gmap[...]
    cell = lax.broadcasted_iota(jnp.int32, (FR, 2 * FW), 1)
    window_parts = split(window)
    for n in range(4):
        chosen = jnp.concatenate(
            [
                jnp.where(
                    jnp.broadcast_to(turned[:, a : a + 1], (FR, 2 * FW)) == cell, 1.0, 0.0
                )
                for a in range(n * 8, n * 8 + 8)
            ],
            axis=0,
        ).astype(jnp.bfloat16)
        total = jnp.zeros((128, 16), jnp.float32)
        for part in window_parts:
            total = total + lax.dot_general(
                chosen, part, (((1,), (1,)), ((), ())), preferred_element_type=jnp.float32
            )
        ghosts[n * 128 : n * 128 + 128, 0:16] = total

    def plane2(a, low, high):
        for half in range(2):
            f = pull_plane(relaxed1, ghosts, 0, a, half, low, high)
            row = pl.multiple_of(a * FR + half * 8, 8)
            push = [force[k, pl.ds(row, 8), :] for k in range(3)]
            keep_plane(relaxed2, a, half, collide(f, push, -0.25))

    def inner2(a, carry):
        plane2(a, None, None)
        return carry

    def rim2(c, carry):
        for r in (0, FR - 1):
            f = pull_rim(relaxed1, back1, forth1, ghosts, 0, c, r, first, last)
            rows = pl.ds(c * (8 * FR) + r, 8, stride=FR)
            push = [force[k, rows, :] for k in range(3)]
            keep_rim(1, relaxed2, c, r, collide(f, push, -0.25))
        return carry

    lax.fori_loop(1, FA - 1, inner2, 0)
    arrive(copies1)
    plane2(0, end_mask(first), None)
    plane2(FA - 1, None, end_mask(last))
    lax.fori_loop(0, 4, rim2, 0)
    copies2 = exchange(1, relaxed2, back2, forth2)
    start(copies2)
    for copy in rims:
        copy.wait_send()
    ghost_copy.wait_send()
    leave(copies1)
    arrive(copies2)
    leave(copies2)


def settle(n_coarse, relaxed, back, forth, ghosts, out_hbm, out, sem):
    p = lax.axis_index("coarse")
    first, last = p == 0, p == n_coarse - 1

    def plane(a, low, high):
        for half in range(2):
            f = pull_plane(relaxed, ghosts, 5, a, half, low, high)
            row = pl.multiple_of(a * FR + half * 8, 8)
            for i in range(19):
                out[i, pl.ds(row, 8), :] = f[i] * 0.0625

    def inner(a, carry):
        plane(a, None, None)
        return carry

    copies = []
    for c in range(4):
        if c == 0:
            plane(0, end_mask(first), None)
        lax.fori_loop(max(c * 8, 1), min(c * 8 + 8, FA - 1), inner, 0)
        if c == 3:
            plane(FA - 1, None, end_mask(last))
        for r in (0, FR - 1):
            f = pull_rim(relaxed, back, forth, ghosts, 5, c, r, first, last)
            for i in range(19):
                out[i, pl.ds(c * (8 * FR) + r, 8, stride=FR), :] = f[i] * 0.0625
        rows = pl.ds(c * 128, 128)
        copy = pltpu.make_async_copy(out.at[:, rows, :], out_hbm.at[:, rows, :], sem.at[c])
        copy.start()
        copies.append(copy)
    for copy in copies:
        copy.wait()


def local(
    fine_populations,
    coarse_face,
    ghost_map,
    marker_force,
    marker_weights,
    marker_tiles,
    block_counts,
):
    n_coarse, n_sector = lax.axis_size("coarse"), lax.axis_size("sector")
    f32 = jnp.float32
    vmem = pl.BlockSpec(memory_space=pltpu.VMEM)
    hbm = pl.BlockSpec(memory_space=pltpu.HBM)
    margin = (5, 48, FW)
    state = pl.pallas_call(
        functools.partial(advance, n_coarse, n_sector),
        out_shape=(
            pltpu.VMEM((19, ROWS, FW), f32),
            pltpu.VMEM(margin, f32),
            pltpu.VMEM(margin, f32),
            pltpu.VMEM((FA * FR, FW), f32),
        ),
        in_specs=[hbm] * 6 + [pl.BlockSpec(memory_space=pltpu.SMEM)],
        out_specs=(vmem, vmem, vmem, vmem),
        scratch_shapes=[
            pltpu.VMEM((19, FA * FR, FW), f32),
            pltpu.VMEM((19, 2, FW), f32),
            pltpu.VMEM((FR, FA), jnp.int32),
            pltpu.VMEM((3, NB, MB), jnp.bfloat16),
            pltpu.VMEM((NB, MB, FW), jnp.bfloat16),
            pltpu.SMEM((NB,), jnp.int32),
            pltpu.VMEM((NB * 8, MB), f32),
            pltpu.VMEM((NB * 8, FW), f32),
            pltpu.VMEM((3, FA * FR + 2 * FA, FW), f32),
            pltpu.VMEM((3, FA, FW), f32),
            pltpu.VMEM((3, FA, FW), f32),
            pltpu.VMEM((16, FW), f32),
            pltpu.VMEM((16, FW), f32),
            pltpu.VMEM((19, ROWS, FW), f32),
            pltpu.VMEM(margin, f32),
            pltpu.VMEM(margin, f32),
            pltpu.VMEM((4, 5, FA, FW), f32),
            pltpu.SemaphoreType.DMA((9,)),
            pltpu.SemaphoreType.DMA((N_REMOTE,)),
            pltpu.SemaphoreType.DMA((N_REMOTE,)),
        ],
        compiler_params=pltpu.CompilerParams(
            collective_id=0, has_side_effects=True, vmem_limit_bytes=32 * 1024 * 1024
        ),
        name="advance",
    )(
        *(
            pltpu.with_memory_space_constraint(x, pltpu.HBM)
            for x in (
                fine_populations.reshape(19, FA * FR, FW),
                jnp.transpose(coarse_face, (1, 0, 2)),
                jnp.transpose(ghost_map),
                jnp.transpose(marker_force, (1, 0, 2)),
                marker_weights,
                marker_tiles,
            )
        ),
        block_counts,
    )
    out = pl.pallas_call(
        functools.partial(settle, n_coarse),
        out_shape=jax.ShapeDtypeStruct((19, FA * FR, FW), f32),
        in_specs=[vmem, vmem, vmem, vmem],
        out_specs=hbm,
        scratch_shapes=[
            pltpu.VMEM((19, FA * FR, FW), f32),
            pltpu.SemaphoreType.DMA((4,)),
        ],
        compiler_params=pltpu.CompilerParams(vmem_limit_bytes=32 * 1024 * 1024),
        name="settle",
    )(*state)
    return out.reshape(19, FA, FR, FW)


def solution(mesh):
    in_specs = (
        P(None, "coarse", "sector", None),
        P(None, None, ("coarse", "sector")),
        P("coarse", "sector"),
        P(("coarse", "sector"), None, None),
        P(("coarse", "sector"), None, None),
        P(("coarse", "sector")),
        P(("coarse", "sector")),
    )
    out_specs = P(None, "coarse", "sector", None)
    return jax.shard_map(local, mesh=mesh, in_specs=in_specs, out_specs=out_specs, check_vma=False)
```

time: 130 us -> 35.2 us (0.27)
  other arithmetic: 43.3 us -> 0 us
  starting transfers between devices: 38.2 us -> 0 us
  Pallas kernels: 0 us -> 34.5 us
  local copies, waits for them, and re-layouts: 26.4 us -> 0 us
  waiting for transfers between devices: 19.1 us -> 0 us
    ppermute x11 -> x0, starting transfers between devices: 38.2 us -> none  [the longest x5 20.9 us: extended(): lax.ppermute(head, axis, [((i + 1) % count, i) for i in range(ends)])]
    pallas_call x0 -> x2, Pallas kernels: none -> 34.5 us  [the longest x1 29.7 us: local(): pl.pallas_call(functools.partial(advance, n_coarse, n_sector), out_shape=...]
    unnamed x49 -> x0, other arithmetic: 28.1 us -> none
    ppermute x11 -> x0, waiting for transfers between devices: 19.1 us -> none  [the longest x5 10.3 us: extended(): lax.ppermute(tail, axis, [(i, (i + 1) % count) for i in range(ends)])]
    slice x17 -> x0, local copies, waits for them, and re-layouts: 8.99 us -> none  [the longest x2 5.25 us: moments(): density = density + populations[pop_index]]
    add x11 -> x0, other arithmetic: 7.53 us -> none  [the longest x3 5.26 us: collide(): populations[pop_index] - (populations[pop_index] - balance) / TAU_FINE]
    unnamed x37 -> x0, local copies, waits for them, and re-layouts: 6.92 us -> none
    scatter-add x2 -> x0, local copies, waits for them, and re-layouts: 5.1 us -> none  [the longest x1 2.55 us: spread_markers(): force_field = force_field.at[:, :, :1].add(arrived[:, :, :1])]
  transfers between devices with their start and end apart: 11 -> 0, of which waited for: 7 -> 0; matrix products, arithmetic and copies ran while one was open for 18% -> 0% of each run, Pallas kernels for 0% -> 0%
where the time goes in v1:
time: 35.2 us; the launch traced here: 35.1 us
  Pallas kernels  34.5 us (98%)
  between operations  0.66 us (2%)
    pallas_call x1, Pallas kernels, local(): pl.pallas_call(functools.partial(advance, n_coarse, n_sector), out_shape=...  29.7 us
    pallas_call x1, Pallas kernels, local(): pl.pallas_call(functools.partial(settle, n_coarse), out_shape=jax.ShapeDt...  4.73 us

profile of v1, /device:TPU:1, one launch (start us, length us, event | category | flops | bytes accessed | tf_op | source)
XLA Modules:
  0.0 35.1 jit_solution(2999608815388673336)
XLA Ops:
  0.7 29.7 %advance.1 = (f32[19,824,128]{2,1,0:T(8,128)S(1)}, f32[5,48,128]{2,1,0:T(8,128)S(1)}, f32[5,48,128]{2,1,0:T(8,128)S(1)}, f32[512,128]{1,0:T(8,128)S(1)}) custom-call(f32[19,512,128]{2,1,0:T(8,128)} %bitcast.5, f32[19,2,128]{2,1,0:T(2,128)} %bitcast.7, s32[16,32]{1,0:T(8,128)} %bitcast.8, bf16[3,32,128]{2,1,0:T(8,128)(2,1)} %bitcast.6, ...), custom_call_target="tpu_custom_call" | custom-call | tf_op jit(solution)/shard_map/advance/pallas_call | solution.py:554
  30.4 4.7 %settle.1 = f32[19,512,128]{2,1,0:T(8,128)} custom-call(f32[19,824,128]{2,1,0:T(8,128)S(1)} %get-tuple-element.9.relaxed, f32[5,48,128]{2,1,0:T(8,128)S(1)} %get-tuple-element.10.back, f32[5,48,128]{2,1,0:T(8,128)S(1)} %get-tuple-element.11.forth, f32[512,128]{1,0:T(8,128)S(1)} %get-tuple-element.12.ghosts), custom_call_target="tpu_custom_call" | custom-call | tf_op jit(solution)/shard_map/settle/pallas_call | solution.py:604

commit v2 on v1

--- a/solution.py
+++ b/solution.py
@@ -42,15 +42,16 @@
 
 UP = [i for i in range(19) if VELOCITIES[i][0] == 1]
 DOWN = [i for i in range(19) if VELOCITIES[i][0] == -1]
-FORTH = [i for i in range(19) if VELOCITIES[i][1] == 1]
-BACK = [i for i in range(19) if VELOCITIES[i][1] == -1]
+FORTH = [3, 15, 17, 10, 7]
+BACK = [4, 16, 18, 8, 9]
 INWARD = [i for i in range(19) if VELOCITIES[i][2] == -1]
 ORDER = UP + DOWN + [i for i in range(19) if VELOCITIES[i][0] == 0]
 SLOT = {pop: slot for slot, pop in enumerate(ORDER)}
 
-RIM_BACK, RIM_FORTH, GHOST = 0, 1, 2
-EXCHANGE = 3
-N_REMOTE = EXCHANGE + 16
+V_AT, INVERSE_AT, RIM_AT, PARTS = 5, 8, 9, 12
+
+GHOST, FIRST, SECOND = 0, 1, 13
+N_REMOTE = SECOND + 8
 
 MESH = pl.DeviceIdType.MESH
 
@@ -97,7 +98,23 @@
         ):
             out[j] = f[j] + (even + odd)
             out[j + 1] = f[j + 1] + (even - odd)
-    return out
+    return out, u, inverse
+
+
+def along(vector, i):
+    terms = [vector[k] if VELOCITIES[i][k] == 1 else -vector[k] for k in range(3) if VELOCITIES[i][k]]
+    return functools.reduce(lambda x, y: x + y, terms)
+
+
+def corrected(base, pops, extra, v, inverse):
+    w = [v[k] + 1.03125 * inverse * extra[k] for k in range(3)]
+    shared = w[0] * extra[0] + w[1] * extra[1] + w[2] * extra[2]
+    values = []
+    for value, i in zip(base, pops):
+        pushed = along(extra, i)
+        grown = 3.0 * (pushed + along(w, i) * pushed) - shared
+        values.append(value - (4.0 * LATTICE_WEIGHTS[i]) * grown)
+    return values
 
 
 def interface_rows(pops):
@@ -160,20 +177,20 @@
     return pulled(load, ghost, first_column, low, high)
 
 
-def pull_rim(relaxed, margin_back, margin_forth, ghosts, first_column, c, r, first, last):
+def pull_rim(relaxed, margin, ghosts, first_column, c, r, first, last):
     row = OFF + c * (8 * PLANE) + r
 
     def load(i, da, dr):
         if r + dr < 0:
-            return margin_back[FORTH.index(i), pl.ds(8 + c * 8 + da, 8), :]
+            return margin[0, FORTH.index(i), pl.ds(8 + c * 8 + da, 8), :]
         if r + dr >= FR:
-            return margin_forth[BACK.index(i), pl.ds(8 + c * 8 + da, 8), :]
+            return margin[1, BACK.index(i), pl.ds(8 + c * 8 + da, 8), :]
         return relaxed[SLOT[i], pl.ds(row + da * PLANE + dr, 8, stride=PLANE), :]
 
     ghost = ghosts[pl.ds(c * (8 * FR) + r, 8, stride=FR), :]
-    along = lax.broadcasted_iota(jnp.int32, (8, FW), 0) + c * 8
-    low = along == jnp.where(first, 0, -1)
-    high = along == jnp.where(last, FA - 1, -1)
+    axial = lax.broadcasted_iota(jnp.int32, (8, FW), 0) + c * 8
+    low = axial == jnp.where(first, 0, -1)
+    high = axial == jnp.where(last, FA - 1, -1)
     return pulled(load, ghost, first_column, low, high)
 
 
@@ -200,8 +217,7 @@
     tiles_hbm,
     count_ref,
     relaxed2,
-    back2,
-    forth2,
+    margin2,
     ghosts,
     fine,
     face,
@@ -212,13 +228,14 @@
     rows3,
     parts,
     force,
-    rim_back,
-    rim_forth,
+    rims,
     gown,
     gnext,
     relaxed1,
-    back1,
-    forth1,
+    margin1,
+    outbox,
+    inbox,
+    edges,
     sends,
     local_sem,
     send_sem,
@@ -303,10 +320,14 @@
         chosen = jnp.where(cell == target, 1.0, 0.0).astype(jnp.bfloat16)
         summed = jnp.dot(chosen, columns, preferred_element_type=jnp.float32)
         for k in range(3):
-            force[k, n * 64 : n * 64 + 64, :] = summed[:, k * FW : k * FW + FW]
-
-    peers = 2 + jnp.where(has_low, 3, 0) + jnp.where(has_high, 3, 0)
-    pl.semaphore_wait(barrier, peers)
+            column = summed[:, k * FW : k * FW + FW]
+            if n < 8:
+                force[k, n * 64 : n * 64 + 64, :] = column
+            else:
+                for side in range(2):
+                    rim = column[side * FA : side * FA + FA]
+                    rims[side, k, 8:40, :] = rim
+                    outbox[side, RIM_AT + k, :, :] = rim
 
     def send(n, src, dst, coarse, sector):
         return pltpu.make_async_remote_copy(
@@ -317,13 +338,6 @@
             device_id={"coarse": coarse, "sector": sector},
             device_id_type=MESH,
         )
-
-    rims = [
-        send(RIM_BACK, force.at[:, 512:544, :], rim_forth, p, behind),
-        send(RIM_FORTH, force.at[:, 544:576, :], rim_back, p, ahead),
-    ]
-    for copy in rims:
-        copy.start()
 
     loads[2].wait()
     for k in range(2):
@@ -336,39 +350,85 @@
     for j in range(10, 16):
         gown[j : j + 1, :] = jnp.zeros((1, FW), jnp.float32)
     ghost_copy = send(GHOST, gown, gnext, p, behind)
-    ghost_copy.start()
-
-    def exchange(k, relaxed, back, forth):
-        base = EXCHANGE + 8 * k
-        top, bottom = OFF + (FA - 1) * PLANE, OFF
-        to_back, to_forth = sends.at[2 * k], sends.at[2 * k + 1]
+    top, bottom = OFF + (FA - 1) * PLANE, OFF
+
+    def planes(n, relaxed):
+        upward = send(
+            n,
+            relaxed.at[0:5, top : top + FR, :],
+            relaxed.at[0:5, bottom - PLANE : bottom - PLANE + FR, :],
+            p + 1,
+            s,
+        )
+        downward = send(
+            n + 1,
+            relaxed.at[5:10, bottom : bottom + FR, :],
+            relaxed.at[5:10, top + PLANE : top + PLANE + FR, :],
+            p - 1,
+            s,
+        )
+        return upward, downward
+
+    def first_exchange():
+        n = FIRST
         both = [
-            send(base, to_forth, back.at[:, 8:40, :], p, ahead),
-            send(base + 1, to_back, forth.at[:, 8:40, :], p, behind),
+            send(n, outbox.at[1], inbox.at[0, :, 8:40, :], p, ahead),
+            send(n + 1, outbox.at[0], inbox.at[1, :, 8:40, :], p, behind),
         ]
-        up7, down10 = FORTH.index(7), FORTH.index(10)
-        up9, down8 = BACK.index(9), BACK.index(8)
+        upward, downward = planes(n + 2, relaxed1)
+        upward, downward = [upward], [downward]
+        for group, m, coarse, low, there, edge in (
+            (upward, n + 4, p + 1, 24, 0, 0),
+            (downward, n + 8, p - 1, 0, 40, 1),
+        ):
+            group += [
+                send(
+                    m,
+                    rims.at[:, :, 8 + low : 16 + low, :],
+                    rims.at[:, :, there : there + 8, :],
+                    coarse,
+                    s,
+                ),
+                send(
+                    m + 1,
+                    outbox.at[:, V_AT:RIM_AT, low : low + 8, :],
+                    edges.at[edge],
+                    coarse,
+                    s,
+                ),
+                send(
+                    m + 2,
+                    outbox.at[1, 3:PARTS, low : low + 8, :],
+                    inbox.at[0, 3:PARTS, there : there + 8, :],
+                    coarse,
+                    ahead,
+                ),
+                send(
+                    m + 3,
+                    outbox.at[0, 3:PARTS, low : low + 8, :],
+                    inbox.at[1, 3:PARTS, there : there + 8, :],
+                    coarse,
+                    behind,
+                ),
+            ]
+        return both, upward, downward
+
+    def second_exchange():
+        n = SECOND
+        both = [
+            send(n, sends.at[1], margin2.at[0, :, 8:40, :], p, ahead),
+            send(n + 1, sends.at[0], margin2.at[1, :, 8:40, :], p, behind),
+        ]
+        upward, downward = planes(n + 2, relaxed2)
         upward = [
-            send(
-                base + 2,
-                relaxed.at[0:5, top : top + FR, :],
-                relaxed.at[0:5, bottom - PLANE : bottom - PLANE + FR, :],
-                p + 1,
-                s,
-            ),
-            send(base + 3, to_forth.at[up7, 24:32, :], back.at[up7, 0:8, :], p + 1, ahead),
-            send(base + 4, to_back.at[up9, 24:32, :], forth.at[up9, 0:8, :], p + 1, behind),
+            upward,
+            send(n + 4, sends.at[1, 4, 24:32, :], margin2.at[0, 4, 0:8, :], p + 1, ahead),
+            send(n + 5, sends.at[0, 4, 24:32, :], margin2.at[1, 4, 0:8, :], p + 1, behind),
         ]
         downward = [
-            send(
-                base + 5,
-                relaxed.at[5:10, bottom : bottom + FR, :],
-                relaxed.at[5:10, top + PLANE : top + PLANE + FR, :],
-                p - 1,
-                s,
-            ),
-            send(base + 6, to_forth.at[down10, 0:8, :], back.at[down10, 40:48, :], p - 1, ahead),
-            send(base + 7, to_back.at[down8, 0:8, :], forth.at[down8, 40:48, :], p - 1, behind),
+            downward,
+            send(n + 6, sends.at[1, 3, 0:8, :], margin2.at[0, 3, 40:48, :], p - 1, ahead),
+            send(n + 7, sends.at[0, 3, 0:8, :], margin2.at[1, 3, 40:48, :], p - 1, behind),
         ]
         return both, upward, downward
 
@@ -405,46 +465,48 @@
                 for copy in group:
                     copy.wait_send()
 
-    def keep_plane(relaxed, a, half, values):
-        row = pl.multiple_of(OFF + a * PLANE + half * 8, 8)
+    def keep_plane(relaxed, a, half, values, inside=False):
+        rows = pl.ds(pl.multiple_of(OFF + a * PLANE + half * 8, 8), 8)
         for i in range(19):
-            relaxed[SLOT[i], pl.ds(row, 8), :] = values[i]
-
-    def keep_rim(k, relaxed, c, r, values):
-        row = OFF + c * (8 * PLANE) + r
-        for i in range(19):
-            relaxed[SLOT[i], pl.ds(row, 8, stride=PLANE), :] = values[i]
-        for j, i in enumerate(BACK if r == 0 else FORTH):
-            side = 2 * k if r == 0 else 2 * k + 1
-            sends[side, j, pl.ds(pl.multiple_of(c * 8, 8), 8), :] = values[i]
+            if inside:
+                row = lax.broadcasted_iota(jnp.int32, (8, FW), 0)
+                pltpu.store(relaxed.at[SLOT[i], rows, :], values[i], mask=row != 7 * half)
+            else:
+                relaxed[SLOT[i], rows, :] = values[i]
 
     def plane1(a, carry):
         for half in range(2):
             row = pl.multiple_of(a * FR + half * 8, 8)
             f = [fine[i, pl.ds(row, 8), :] for i in range(19)]
             push = [force[k, pl.ds(row, 8), :] for k in range(3)]
-            keep_plane(relaxed1, a, half, collide(f, push, 1.0))
+            keep_plane(relaxed1, a, half, collide(f, push, 1.0)[0])
         return carry
 
-    def rim1(c, carry):
-        for r, rim in ((0, rim_back), (FR - 1, rim_forth)):
+    def rim0(c):
+        for side, r in ((0, 0), (1, FR - 1)):
             rows = pl.ds(c * (8 * FR) + r, 8, stride=FR)
             f = [fine[i, rows, :] for i in range(19)]
-            along = pl.ds(pl.multiple_of(c * 8, 8), 8)
-            push = [force[k, rows, :] + rim[k, along, :] for k in range(3)]
+            push = [force[k, rows, :] for k in range(3)]
+            values, u, inverse = collide(f, push, 1.0)
+            cells = slice(c * 8, c * 8 + 8)
+            for j, i in enumerate(FORTH if side else BACK):
+                outbox[side, j, cells, :] = values[i]
             for k in range(3):
-                force[k, rows, :] = push[k]
-            keep_rim(0, relaxed1, c, r, collide(f, push, 1.0))
-        return carry
+                outbox[side, V_AT + k, cells, :] = 3.0 * u[k] + 0.5625 * inverse * push[k]
+            outbox[side, INVERSE_AT, cells, :] = inverse
 
     for c in range(4):
         loads[5 + c].wait()
-        lax.fori_loop(c * 8, c * 8 + 8, plane1, 0)
-    for copy in rims:
-        copy.wait_recv()
-    lax.fori_loop(0, 4, rim1, 0)
-    copies1 = exchange(0, relaxed1, back1, forth1)
+        rim0(c)
+    plane1(0, 0)
+    plane1(FA - 1, 0)
+
+    peers = 2 + jnp.where(has_low, 3, 0) + jnp.where(has_high, 3, 0)
+    pl.semaphore_wait(barrier, peers)
+    ghost_copy.start()
+    copies1 = first_exchange()
     start(copies1)
+    lax.fori_loop(1, FA - 1, plane1, 0, unroll=2)
 
     loads[3].wait()
     ghost_copy.wait_recv()
@@ -469,41 +531,83 @@
             )
         ghosts[n * 128 : n * 128 + 128, 0:16] = total
 
-    def plane2(a, low, high):
+    def plane2(a, low, high, inside=False):
         for half in range(2):
             f = pull_plane(relaxed1, ghosts, 0, a, half, low, high)
             row = pl.multiple_of(a * FR + half * 8, 8)
             push = [force[k, pl.ds(row, 8), :] for k in range(3)]
-            keep_plane(relaxed2, a, half, collide(f, push, -0.25))
+            keep_plane(relaxed2, a, half, collide(f, push, -0.25)[0], inside)
 
     def inner2(a, carry):
-        plane2(a, None, None)
+        plane2(a, None, None, inside=True)
         return carry
 
-    def rim2(c, carry):
-        for r in (0, FR - 1):
-            f = pull_rim(relaxed1, back1, forth1, ghosts, 0, c, r, first, last)
+    def keep_rim(relaxed, c, r, values):
+        row = OFF + c * (8 * PLANE) + r
+        for i in range(19):
+            relaxed[SLOT[i], pl.ds(row, 8, stride=PLANE), :] = values[i]
+
+    def rim1(c):
+        for side, r in ((0, 0), (1, FR - 1)):
+            rows = pl.ds(c * (8 * FR) + r, 8, stride=FR)
+            f = [fine[i, rows, :] for i in range(19)]
+            cells = slice(8 + c * 8, 16 + c * 8)
+            push = [force[k, rows, :] + inbox[side, RIM_AT + k, cells, :] for k in range(3)]
+            for k in range(3):
+                force[k, rows, :] = push[k]
+            keep_rim(relaxed1, c, r, collide(f, push, 1.0)[0])
+
+    def rim2(c):
+        for side, r in ((0, 0), (1, FR - 1)):
+            f = pull_rim(relaxed1, margin1, ghosts, 0, c, r, first, last)
             rows = pl.ds(c * (8 * FR) + r, 8, stride=FR)
             push = [force[k, rows, :] for k in range(3)]
-            keep_rim(1, relaxed2, c, r, collide(f, push, -0.25))
-        return carry
-
-    lax.fori_loop(1, FA - 1, inner2, 0)
+            values = collide(f, push, -0.25)[0]
+            keep_rim(relaxed2, c, r, values)
+            for j, i in enumerate(FORTH if side else BACK):
+                sends[side, j, c * 8 : c * 8 + 8, :] = values[i]
+
     arrive(copies1)
+    leave(copies1)
+    for c in range(4):
+        rim1(c)
+    for side in range(2):
+        for c in range(6):
+            cells = slice(c * 8, c * 8 + 8)
+            values = corrected(
+                [inbox[side, j, cells, :] for j in range(5)],
+                BACK if side else FORTH,
+                [rims[side, k, cells, :] for k in range(3)],
+                [inbox[side, V_AT + k, cells, :] for k in range(3)],
+                inbox[side, INVERSE_AT, cells, :],
+            )
+            for j in range(5):
+                margin1[side, j, cells, :] = values[j]
+    for edge, pops, plane, at, near in ((0, UP, -1, 7, 7), (1, DOWN, FA, 40, 0)):
+        for side, r in ((0, 0), (1, FR - 1)):
+            row = OFF + plane * PLANE + r
+            values = corrected(
+                [relaxed1[SLOT[i], row : row + 1, :] for i in pops],
+                pops,
+                [inbox[side, RIM_AT + k, at : at + 1, :] for k in range(3)],
+                [edges[edge, side, k, near : near + 1, :] for k in range(3)],
+                edges[edge, side, 3, near : near + 1, :],
+            )
+            for i, value in zip(pops, values):
+                relaxed1[SLOT[i], row : row + 1, :] = value
     plane2(0, end_mask(first), None)
     plane2(FA - 1, None, end_mask(last))
-    lax.fori_loop(0, 4, rim2, 0)
-    copies2 = exchange(1, relaxed2, back2, forth2)
+    for c in range(4):
+        rim2(c)
+    copies2 = second_exchange()
     start(copies2)
-    for copy in rims:
-        copy.wait_send()
+    lax.fori_loop(1, FA - 1, inner2, 0, unroll=5)
     ghost_copy.wait_send()
-    leave(copies1)
     arrive(copies2)
     leave(copies2)
 
 
-def settle(n_coarse, relaxed, back, forth, ghosts, out_hbm, out, sem):
+def settle(n_coarse, relaxed, margin, ghosts, out_hbm, out, sem):
     p = lax.axis_index("coarse")
     first, last = p == 0, p == n_coarse - 1
 
@@ -522,11 +626,11 @@
     for c in range(4):
         if c == 0:
             plane(0, end_mask(first), None)
-        lax.fori_loop(max(c * 8, 1), min(c * 8 + 8, FA - 1), inner, 0)
+        lax.fori_loop(max(c * 8, 1), min(c * 8 + 8, FA - 1), inner, 0, unroll=True)
         if c == 3:
             plane(FA - 1, None, end_mask(last))
         for r in (0, FR - 1):
-            f = pull_rim(relaxed, back, forth, ghosts, 5, c, r, first, last)
+            f = pull_rim(relaxed, margin, ghosts, 5, c, r, first, last)
             for i in range(19):
                 out[i, pl.ds(c * (8 * FR) + r, 8, stride=FR), :] = f[i] * 0.0625
         rows = pl.ds(c * 128, 128)
@@ -550,17 +654,16 @@
     f32 = jnp.float32
     vmem = pl.BlockSpec(memory_space=pltpu.VMEM)
     hbm = pl.BlockSpec(memory_space=pltpu.HBM)
-    margin = (5, 48, FW)
+    margin = (2, 5, 48, FW)
     state = pl.pallas_call(
         functools.partial(advance, n_coarse, n_sector),
         out_shape=(
             pltpu.VMEM((19, ROWS, FW), f32),
             pltpu.VMEM(margin, f32),
-            pltpu.VMEM(margin, f32),
             pltpu.VMEM((FA * FR, FW), f32),
         ),
         in_specs=[hbm] * 6 + [pl.BlockSpec(memory_space=pltpu.SMEM)],
-        out_specs=(vmem, vmem, vmem, vmem),
+        out_specs=(vmem, vmem, vmem),
         scratch_shapes=[
             pltpu.VMEM((19, FA * FR, FW), f32),
             pltpu.VMEM((19, 2, FW), f32),
@@ -570,15 +673,16 @@
             pltpu.SMEM((NB,), jnp.int32),
             pltpu.VMEM((NB * 8, MB), f32),
             pltpu.VMEM((NB * 8, FW), f32),
-            pltpu.VMEM((3, FA * FR + 2 * FA, FW), f32),
-            pltpu.VMEM((3, FA, FW), f32),
-            pltpu.VMEM((3, FA, FW), f32),
+            pltpu.VMEM((3, FA * FR, FW), f32),
+            pltpu.VMEM((2, 3, 48, FW), f32),
             pltpu.VMEM((16, FW), f32),
             pltpu.VMEM((16, FW), f32),
             pltpu.VMEM((19, ROWS, FW), f32),
             pltpu.VMEM(margin, f32),
-            pltpu.VMEM(margin, f32),
-            pltpu.VMEM((4, 5, FA, FW), f32),
+            pltpu.VMEM((2, PARTS, FA, FW), f32),
+            pltpu.VMEM((2, PARTS, 48, FW), f32),
+            pltpu.VMEM((2, 2, 4, 8, FW), f32),
+            pltpu.VMEM((2, 5, FA, FW), f32),
             pltpu.SemaphoreType.DMA((9,)),
             pltpu.SemaphoreType.DMA((N_REMOTE,)),
             pltpu.SemaphoreType.DMA((N_REMOTE,)),
@@ -604,7 +708,7 @@
     out = pl.pallas_call(
         functools.partial(settle, n_coarse),
         out_shape=jax.ShapeDtypeStruct((19, FA * FR, FW), f32),
-        in_specs=[vmem, vmem, vmem, vmem],
+        in_specs=[vmem, vmem, vmem],
         out_specs=hbm,
         scratch_shapes=[
             pltpu.VMEM((19, FA * FR, FW), f32),

time: 35.2 us -> 32.3 us (0.918)
  Pallas kernels: 34.5 us -> 31.5 us
    pallas_call x1, Pallas kernels: 4.73 us -> 2.7 us  [local(): pl.pallas_call(functools.partial(settle, n_coarse), out_shape=jax.ShapeDt...]
    pallas_call x1, Pallas kernels: 29.7 us -> 28.8 us  [local(): pl.pallas_call(functools.partial(advance, n_coarse, n_sector), out_shape=...]
where the time goes in v2:
time: 32.3 us; the launch traced here: 32.2 us
  Pallas kernels  31.5 us (98%)
  between operations  0.66 us (2%)
    pallas_call x1, Pallas kernels, local(): pl.pallas_call(functools.partial(advance, n_coarse, n_sector), out_shape=...  28.8 us
    pallas_call x1, Pallas kernels, local(): pl.pallas_call(functools.partial(settle, n_coarse), out_shape=jax.ShapeDt...  2.7 us

profile of v2, /device:TPU:1, one launch (start us, length us, event | category | flops | bytes accessed | tf_op | source)
XLA Modules:
  0.0 32.2 jit_solution(14153469703138296346)
XLA Ops:
  0.7 28.8 %advance.1 = (f32[19,824,128]{2,1,0:T(8,128)S(1)}, f32[2,5,48,128]{3,2,1,0:T(8,128)S(1)}, f32[512,128]{1,0:T(8,128)S(1)}) custom-call(f32[19,512,128]{2,1,0:T(8,128)} %bitcast.5, f32[19,2,128]{2,1,0:T(2,128)} %bitcast.7, s32[16,32]{1,0:T(8,128)} %bitcast.8, bf16[3,32,128]{2,1,0:T(8,128)(2,1)} %bitcast.6, bf16[32,128,128]{2,1,0:T(8,128)(2,1)} %mweights_hbm.1, ...), custom_call_target="tpu_custom_call" | custom-call | tf_op jit(solution)/shard_map/advance/pallas_call | solution.py:658
  29.5 2.7 %settle.1 = f32[19,512,128]{2,1,0:T(8,128)} custom-call(f32[19,824,128]{2,1,0:T(8,128)S(1)} %get-tuple-element.8.relaxed, f32[2,5,48,128]{3,2,1,0:T(8,128)S(1)} %get-tuple-element.9.margin, f32[512,128]{1,0:T(8,128)S(1)} %get-tuple-element.10.ghosts), custom_call_target="tpu_custom_call" | custom-call | tf_op jit(solution)/shard_map/settle/pallas_call | solution.py:708

commit v3 on v2

--- a/solution.py
+++ b/solution.py
@@ -50,8 +50,9 @@
 
 V_AT, INVERSE_AT, RIM_AT, PARTS = 5, 8, 9, 12
 
-GHOST, FIRST, SECOND = 0, 1, 13
-N_REMOTE = SECOND + 8
+GHOST, FIRST, SECOND = 0, 1, 19
+N_REMOTE = SECOND + 14
+CHUNKS = 4
 
 MESH = pl.DeviceIdType.MESH
 
@@ -369,101 +370,71 @@
         )
         return upward, downward
 
-    def first_exchange():
-        n = FIRST
-        both = [
-            send(n, outbox.at[1], inbox.at[0, :, 8:40, :], p, ahead),
-            send(n + 1, outbox.at[0], inbox.at[1, :, 8:40, :], p, behind),
-        ]
-        upward, downward = planes(n + 2, relaxed1)
-        upward, downward = [upward], [downward]
-        for group, m, coarse, low, there, edge in (
-            (upward, n + 4, p + 1, 24, 0, 0),
-            (downward, n + 8, p - 1, 0, 40, 1),
+    def sides(n, box, there):
+        groups = []
+        for c in range(CHUNKS):
+            at, to = pl.ds(c * 8, 8), pl.ds(8 + c * 8, 8)
+            groups.append(
+                [
+                    send(n + 2 * c, box.at[1, :, at, :], there.at[0, :, to, :], p, ahead),
+                    send(n + 2 * c + 1, box.at[0, :, at, :], there.at[1, :, to, :], p, behind),
+                ]
+            )
+        return groups
+
+    def start(group):
+        for copy in group:
+            copy.start()
+
+    def arrive(group):
+        for copy in group:
+            copy.wait_recv()
+
+    def leave(group):
+        for copy in group:
+            copy.wait_send()
+
+    def axially(act, upward, downward, receiving):
+        for there, group in (
+            (has_low if receiving else has_high, upward),
+            (has_high if receiving else has_low, downward),
         ):
-            group += [
-                send(
-                    m,
-                    rims.at[:, :, 8 + low : 16 + low, :],
-                    rims.at[:, :, there : there + 8, :],
-                    coarse,
-                    s,
-                ),
-                send(
-                    m + 1,
-                    outbox.at[:, V_AT:RIM_AT, low : low + 8, :],
-                    edges.at[edge],
-                    coarse,
-                    s,
-                ),
-                send(
-                    m + 2,
-                    outbox.at[1, 3:PARTS, low : low + 8, :],
-                    inbox.at[0, 3:PARTS, there : there + 8, :],
-                    coarse,
-                    ahead,
-                ),
-                send(
-                    m + 3,
-                    outbox.at[0, 3:PARTS, low : low + 8, :],
-                    inbox.at[1, 3:PARTS, there : there + 8, :],
-                    coarse,
-                    behind,
-                ),
-            ]
-        return both, upward, downward
-
-    def second_exchange():
-        n = SECOND
-        both = [
-            send(n, sends.at[1], margin2.at[0, :, 8:40, :], p, ahead),
-            send(n + 1, sends.at[0], margin2.at[1, :, 8:40, :], p, behind),
-        ]
-        upward, downward = planes(n + 2, relaxed2)
-        upward = [
-            upward,
-            send(n + 4, sends.at[1, 4, 24:32, :], margin2.at[0, 4, 0:8, :], p + 1, ahead),
-            send(n + 5, sends.at[0, 4, 24:32, :], margin2.at[1, 4, 0:8, :], p + 1, behind),
-        ]
-        downward = [
-            downward,
-            send(n + 6, sends.at[1, 3, 0:8, :], margin2.at[0, 3, 40:48, :], p - 1, ahead),
-            send(n + 7, sends.at[0, 3, 0:8, :], margin2.at[1, 3, 40:48, :], p - 1, behind),
-        ]
-        return both, upward, downward
-
-    def start(copies):
-        both, upward, downward = copies
-        for copy in both:
-            copy.start()
-        for there, group in ((has_high, upward), (has_low, downward)):
 
             @pl.when(there)
             def _():
-                for copy in group:
-                    copy.start()
-
-    def arrive(copies):
-        both, upward, downward = copies
-        for copy in both:
-            copy.wait_recv()
-        for there, group in ((has_low, upward), (has_high, downward)):
-
-            @pl.when(there)
-            def _():
-                for copy in group:
-                    copy.wait_recv()
-
-    def leave(copies):
-        both, upward, downward = copies
-        for copy in both:
-            copy.wait_send()
-        for there, group in ((has_high, upward), (has_low, downward)):
-
-            @pl.when(there)
-            def _():
-                for copy in group:
-                    copy.wait_send()
+                act(group)
+
+    sides1 = sides(FIRST, outbox, inbox)
+    n = FIRST + 2 * CHUNKS
+    plane_up1, plane_down1 = planes(n, relaxed1)
+    small_up, small_down = [], []
+    for group, m, coarse, row, there, edge in (
+        (small_up, n + 2, p + 1, FA - 1, 7, 0),
+        (small_down, n + 6, p - 1, 0, 40, 1),
+    ):
+        at = pl.ds(row, 1)
+        to = pl.ds(there, 1)
+        group += [
+            send(m, outbox.at[1, 3:PARTS, at, :], inbox.at[0, 3:PARTS, to, :], coarse, ahead),
+            send(m + 1, outbox.at[0, 3:PARTS, at, :], inbox.at[1, 3:PARTS, to, :], coarse, behind),
+            send(m + 2, outbox.at[:, RIM_AT:PARTS, at, :], rims.at[:, :, to, :], coarse, s),
+            send(m + 3, outbox.at[:, V_AT:RIM_AT, at, :], edges.at[edge], coarse, s),
+        ]
+
+    sides2 = sides(SECOND, sends, margin2)
+    n = SECOND + 2 * CHUNKS
+    plane_up2, plane_down2 = planes(n, relaxed2)
+    corners_up, corners_down = [], []
+    for group, m, coarse, row, there, j in (
+        (corners_up, n + 2, p + 1, FA - 1, 7, 4),
+        (corners_down, n + 4, p - 1, 0, 40, 3),
+    ):
+        at = pl.ds(row, 1)
+        to = pl.ds(there, 1)
+        group += [
+            send(m, sends.at[1, j, at, :], margin2.at[0, j, to, :], coarse, ahead),
+            send(m + 1, sends.at[0, j, at, :], margin2.at[1, j, to, :], coarse, behind),
+        ]
 
     def keep_plane(relaxed, a, half, values, inside=False):
         rows = pl.ds(pl.multiple_of(OFF + a * PLANE + half * 8, 8), 8)
@@ -504,8 +475,10 @@
     peers = 2 + jnp.where(has_low, 3, 0) + jnp.where(has_high, 3, 0)
     pl.semaphore_wait(barrier, peers)
     ghost_copy.start()
-    copies1 = first_exchange()
-    start(copies1)
+    axially(start, small_up, small_down, False)
+    for group in sides1:
+        start(group)
+    axially(start, [plane_up1], [plane_down1], False)
     lax.fori_loop(1, FA - 1, plane1, 0, unroll=2)
 
     loads[3].wait()
@@ -531,15 +504,15 @@
             )
         ghosts[n * 128 : n * 128 + 128, 0:16] = total
 
-    def plane2(a, low, high, inside=False):
+    def plane2(a, low, high):
         for half in range(2):
             f = pull_plane(relaxed1, ghosts, 0, a, half, low, high)
             row = pl.multiple_of(a * FR + half * 8, 8)
             push = [force[k, pl.ds(row, 8), :] for k in range(3)]
-            keep_plane(relaxed2, a, half, collide(f, push, -0.25)[0], inside)
+            keep_plane(relaxed2, a, half, collide(f, push, -0.25)[0], True)
 
     def inner2(a, carry):
-        plane2(a, None, None, inside=True)
+        plane2(a, None, None)
         return carry
 
     def keep_rim(relaxed, c, r, values):
@@ -567,44 +540,67 @@
             for j, i in enumerate(FORTH if side else BACK):
                 sends[side, j, c * 8 : c * 8 + 8, :] = values[i]
 
-    arrive(copies1)
-    leave(copies1)
-    for c in range(4):
-        rim1(c)
-    for side in range(2):
-        for c in range(6):
-            cells = slice(c * 8, c * 8 + 8)
-            values = corrected(
-                [inbox[side, j, cells, :] for j in range(5)],
-                BACK if side else FORTH,
-                [rims[side, k, cells, :] for k in range(3)],
-                [inbox[side, V_AT + k, cells, :] for k in range(3)],
-                inbox[side, INVERSE_AT, cells, :],
-            )
-            for j in range(5):
-                margin1[side, j, cells, :] = values[j]
-    for edge, pops, plane, at, near in ((0, UP, -1, 7, 7), (1, DOWN, FA, 40, 0)):
+    def margin_rows(side, cells, which):
+        pops = [(BACK if side else FORTH)[j] for j in which]
+        values = corrected(
+            [inbox[side, j, cells, :] for j in which],
+            pops,
+            [rims[side, k, cells, :] for k in range(3)],
+            [inbox[side, V_AT + k, cells, :] for k in range(3)],
+            inbox[side, INVERSE_AT, cells, :],
+        )
+        for j, value in zip(which, values):
+            margin1[side, j, cells, :] = value
+
+    def edge_rows(edge, pops, plane, at):
         for side, r in ((0, 0), (1, FR - 1)):
             row = OFF + plane * PLANE + r
             values = corrected(
                 [relaxed1[SLOT[i], row : row + 1, :] for i in pops],
                 pops,
                 [inbox[side, RIM_AT + k, at : at + 1, :] for k in range(3)],
-                [edges[edge, side, k, near : near + 1, :] for k in range(3)],
-                edges[edge, side, 3, near : near + 1, :],
+                [edges[edge, side, k, :, :] for k in range(3)],
+                edges[edge, side, 3, :, :],
             )
             for i, value in zip(pops, values):
                 relaxed1[SLOT[i], row : row + 1, :] = value
+
+    axially(arrive, [plane_up1], [plane_down1], True)
+    axially(leave, [plane_up1], [plane_down1], False)
+    axially(arrive, small_up, small_down, True)
+    for side in range(2):
+        margin_rows(side, slice(7, 8), [4])
+        margin_rows(side, slice(40, 41), [3])
+    edge_rows(0, UP, -1, 7)
+    edge_rows(1, DOWN, FA, 40)
+    for c in range(CHUNKS):
+        arrive(sides1[c])
+        rim1(c)
+        for side in range(2):
+            margin_rows(side, slice(8 + c * 8, 16 + c * 8), range(5))
+        ready = [c - 1] if c > 0 else []
+        if c == CHUNKS - 1:
+            ready.append(c)
+        for done in ready:
+            rim2(done)
+            start(sides2[done])
+            if done == 0:
+                axially(start, [], corners_down, False)
+    axially(start, corners_up, [], False)
     plane2(0, end_mask(first), None)
     plane2(FA - 1, None, end_mask(last))
-    for c in range(4):
-        rim2(c)
-    copies2 = second_exchange()
-    start(copies2)
+    axially(start, [plane_up2], [plane_down2], False)
     lax.fori_loop(1, FA - 1, inner2, 0, unroll=5)
     ghost_copy.wait_send()
-    arrive(copies2)
-    leave(copies2)
+    for group in sides1:
+        leave(group)
+    axially(leave, small_up, small_down, False)
+    axially(arrive, [plane_up2] + corners_up, [plane_down2] + corners_down, True)
+    for group in sides2:
+        arrive(group)
+    for group in sides2:
+        leave(group)
+    axially(leave, [plane_up2] + corners_up, [plane_down2] + corners_down, False)
 
 
 def settle(n_coarse, relaxed, margin, ghosts, out_hbm, out, sem):
@@ -681,7 +677,7 @@
             pltpu.VMEM(margin, f32),
             pltpu.VMEM((2, PARTS, FA, FW), f32),
             pltpu.VMEM((2, PARTS, 48, FW), f32),
-            pltpu.VMEM((2, 2, 4, 8, FW), f32),
+            pltpu.VMEM((2, 2, 4, 1, FW), f32),
             pltpu.VMEM((2, 5, FA, FW), f32),
             pltpu.SemaphoreType.DMA((9,)),
             pltpu.SemaphoreType.DMA((N_REMOTE,)),

time: 32.3 us -> 29.9 us (0.926)
  Pallas kernels: 31.5 us -> 29.1 us
    pallas_call x1, Pallas kernels: 28.8 us -> 26.4 us  [local(): pl.pallas_call(functools.partial(advance, n_coarse, n_sector), out_shape=...]
where the time goes in v3:
time: 29.9 us; the launch traced here: 29.8 us
  Pallas kernels  29.1 us (97%)
  between operations  0.66 us (2%)
    pallas_call x1, Pallas kernels, local(): pl.pallas_call(functools.partial(advance, n_coarse, n_sector), out_shape=...  26.4 us
    pallas_call x1, Pallas kernels, local(): pl.pallas_call(functools.partial(settle, n_coarse), out_shape=jax.ShapeDt...  2.7 us

profile of v3, /device:TPU:1, one launch (start us, length us, event | category | flops | bytes accessed | tf_op | source)
XLA Modules:
  0.0 29.8 jit_solution(2761116619266490493)
XLA Ops:
  0.7 26.4 %advance.1 = (f32[19,824,128]{2,1,0:T(8,128)S(1)}, f32[2,5,48,128]{3,2,1,0:T(8,128)S(1)}, f32[512,128]{1,0:T(8,128)S(1)}) custom-call(f32[19,512,128]{2,1,0:T(8,128)} %bitcast.5, f32[19,2,128]{2,1,0:T(2,128)} %bitcast.7, s32[16,32]{1,0:T(8,128)} %bitcast.8, bf16[3,32,128]{2,1,0:T(8,128)(2,1)} %bitcast.6, bf16[32,128,128]{2,1,0:T(8,128)(2,1)} %mweights_hbm.1, ...), custom_call_target="tpu_custom_call" | custom-call | tf_op jit(solution)/shard_map/advance/pallas_call | solution.py:654
  27.1 2.7 %settle.1 = f32[19,512,128]{2,1,0:T(8,128)} custom-call(f32[19,824,128]{2,1,0:T(8,128)S(1)} %get-tuple-element.8.relaxed, f32[2,5,48,128]{3,2,1,0:T(8,128)S(1)} %get-tuple-element.9.margin, f32[512,128]{1,0:T(8,128)S(1)} %get-tuple-element.10.ghosts), custom_call_target="tpu_custom_call" | custom-call | tf_op jit(solution)/shard_map/settle/pallas_call | solution.py:704

commit v4 on v3

--- a/solution.py
+++ b/solution.py
@@ -581,12 +581,13 @@
         ready = [c - 1] if c > 0 else []
         if c == CHUNKS - 1:
             ready.append(c)
-        for done in ready:
+        for done in ready[::-1]:
             rim2(done)
-            start(sides2[done])
             if done == 0:
                 axially(start, [], corners_down, False)
-    axially(start, corners_up, [], False)
+            if done == CHUNKS - 1:
+                axially(start, corners_up, [], False)
+            start(sides2[done])
     plane2(0, end_mask(first), None)
     plane2(FA - 1, None, end_mask(last))
     axially(start, [plane_up2], [plane_down2], False)

time: 29.9 us -> 29.1 us (0.973)
  Pallas kernels: 29.1 us -> 28.4 us
    pallas_call x1, Pallas kernels: 26.4 us -> 25.7 us  [local(): pl.pallas_call(functools.partial(advance, n_coarse, n_sector), out_shape=...]
where the time goes in v4:
time: 29.1 us; the launch traced here: 29 us
  Pallas kernels  28.4 us (98%)
  between operations  0.66 us (2%)
    pallas_call x1, Pallas kernels, local(): pl.pallas_call(functools.partial(advance, n_coarse, n_sector), out_shape=...  25.7 us
    pallas_call x1, Pallas kernels, local(): pl.pallas_call(functools.partial(settle, n_coarse), out_shape=jax.ShapeDt...  2.7 us

profile of v4, /device:TPU:1, one launch (start us, length us, event | category | flops | bytes accessed | tf_op | source)
XLA Modules:
  0.0 29.0 jit_solution(12189519684709192917)
XLA Ops:
  0.7 25.7 %advance.1 = (f32[19,824,128]{2,1,0:T(8,128)S(1)}, f32[2,5,48,128]{3,2,1,0:T(8,128)S(1)}, f32[512,128]{1,0:T(8,128)S(1)}) custom-call(f32[19,512,128]{2,1,0:T(8,128)} %bitcast.5, f32[19,2,128]{2,1,0:T(2,128)} %bitcast.7, s32[16,32]{1,0:T(8,128)} %bitcast.8, bf16[3,32,128]{2,1,0:T(8,128)(2,1)} %bitcast.6, bf16[32,128,128]{2,1,0:T(8,128)(2,1)} %mweights_hbm.1, ...), custom_call_target="tpu_custom_call" | custom-call | tf_op jit(solution)/shard_map/advance/pallas_call | solution.py:655
  26.3 2.7 %settle.1 = f32[19,512,128]{2,1,0:T(8,128)} custom-call(f32[19,824,128]{2,1,0:T(8,128)S(1)} %get-tuple-element.8.relaxed, f32[2,5,48,128]{3,2,1,0:T(8,128)S(1)} %get-tuple-element.9.margin, f32[512,128]{1,0:T(8,128)S(1)} %get-tuple-element.10.ghosts), custom_call_target="tpu_custom_call" | custom-call | tf_op jit(solution)/shard_map/settle/pallas_call | solution.py:705

commit v5 on v3

--- a/solution.py
+++ b/solution.py
@@ -53,6 +53,9 @@
 GHOST, FIRST, SECOND = 0, 1, 19
 N_REMOTE = SECOND + 14
 CHUNKS = 4
+FIRST_ROWS = ((0, 9), (9, 8), (17, 6), (23, 9))
+FIRST_STARTS = ((0, 1), (9,), (16,), (23, 24))
+ALIGNED_ROWS = ((0, 8), (8, 8), (16, 8), (24, 8))
 
 MESH = pl.DeviceIdType.MESH
 
@@ -370,10 +373,10 @@
         )
         return upward, downward
 
-    def sides(n, box, there):
+    def sides(n, box, there, chunks):
         groups = []
-        for c in range(CHUNKS):
-            at, to = pl.ds(c * 8, 8), pl.ds(8 + c * 8, 8)
+        for c, (row, size) in enumerate(chunks):
+            at, to = pl.ds(row, size), pl.ds(8 + row, size)
             groups.append(
                 [
                     send(n + 2 * c, box.at[1, :, at, :], there.at[0, :, to, :], p, ahead),
@@ -404,7 +407,7 @@
             def _():
                 act(group)
 
-    sides1 = sides(FIRST, outbox, inbox)
+    sides1 = sides(FIRST, outbox, inbox, FIRST_ROWS)
     n = FIRST + 2 * CHUNKS
     plane_up1, plane_down1 = planes(n, relaxed1)
     small_up, small_down = [], []
@@ -421,7 +424,7 @@
             send(m + 3, outbox.at[:, V_AT:RIM_AT, at, :], edges.at[edge], coarse, s),
         ]
 
-    sides2 = sides(SECOND, sends, margin2)
+    sides2 = sides(SECOND, sends, margin2, ALIGNED_ROWS)
     n = SECOND + 2 * CHUNKS
     plane_up2, plane_down2 = planes(n, relaxed2)
     corners_up, corners_down = [], []
@@ -476,8 +479,8 @@
     pl.semaphore_wait(barrier, peers)
     ghost_copy.start()
     axially(start, small_up, small_down, False)
-    for group in sides1:
-        start(group)
+    for c in (0, 3, 1, 2):
+        start(sides1[c])
     axially(start, [plane_up1], [plane_down1], False)
     lax.fori_loop(1, FA - 1, plane1, 0, unroll=2)
 
@@ -515,28 +518,27 @@
         plane2(a, None, None)
         return carry
 
-    def keep_rim(relaxed, c, r, values):
-        row = OFF + c * (8 * PLANE) + r
+    def keep_rim(relaxed, a, r, values):
+        row = OFF + a * PLANE + r
         for i in range(19):
             relaxed[SLOT[i], pl.ds(row, 8, stride=PLANE), :] = values[i]
 
-    def rim1(c):
+    def whole_force(side, a, rows):
+        cells = slice(8 + a, 16 + a)
+        return [force[k, rows, :] + inbox[side, RIM_AT + k, cells, :] for k in range(3)]
+
+    def rim1(a):
         for side, r in ((0, 0), (1, FR - 1)):
-            rows = pl.ds(c * (8 * FR) + r, 8, stride=FR)
+            rows = pl.ds(a * FR + r, 8, stride=FR)
             f = [fine[i, rows, :] for i in range(19)]
-            cells = slice(8 + c * 8, 16 + c * 8)
-            push = [force[k, rows, :] + inbox[side, RIM_AT + k, cells, :] for k in range(3)]
-            for k in range(3):
-                force[k, rows, :] = push[k]
-            keep_rim(relaxed1, c, r, collide(f, push, 1.0)[0])
+            keep_rim(relaxed1, a, r, collide(f, whole_force(side, a, rows), 1.0)[0])
 
     def rim2(c):
         for side, r in ((0, 0), (1, FR - 1)):
             f = pull_rim(relaxed1, margin1, ghosts, 0, c, r, first, last)
             rows = pl.ds(c * (8 * FR) + r, 8, stride=FR)
-            push = [force[k, rows, :] for k in range(3)]
-            values = collide(f, push, -0.25)[0]
-            keep_rim(relaxed2, c, r, values)
+            values = collide(f, whole_force(side, c * 8, rows), -0.25)[0]
+            keep_rim(relaxed2, c * 8, r, values)
             for j, i in enumerate(FORTH if side else BACK):
                 sends[side, j, c * 8 : c * 8 + 8, :] = values[i]
 
@@ -567,26 +569,31 @@
 
     axially(arrive, [plane_up1], [plane_down1], True)
     axially(leave, [plane_up1], [plane_down1], False)
+    def take(c):
+        arrive(sides1[c])
+        for a in FIRST_STARTS[c]:
+            rim1(a)
+            for side in range(2):
+                margin_rows(side, slice(8 + a, 16 + a), range(5))
+
+    take(0)
+    take(3)
     axially(arrive, small_up, small_down, True)
     for side in range(2):
         margin_rows(side, slice(7, 8), [4])
         margin_rows(side, slice(40, 41), [3])
     edge_rows(0, UP, -1, 7)
     edge_rows(1, DOWN, FA, 40)
-    for c in range(CHUNKS):
-        arrive(sides1[c])
-        rim1(c)
-        for side in range(2):
-            margin_rows(side, slice(8 + c * 8, 16 + c * 8), range(5))
-        ready = [c - 1] if c > 0 else []
-        if c == CHUNKS - 1:
-            ready.append(c)
-        for done in ready:
-            rim2(done)
-            start(sides2[done])
-            if done == 0:
-                axially(start, [], corners_down, False)
+    rim2(0)
+    axially(start, [], corners_down, False)
+    start(sides2[0])
+    rim2(3)
     axially(start, corners_up, [], False)
+    start(sides2[3])
+    for c in (1, 2):
+        take(c)
+        rim2(c)
+        start(sides2[c])
     plane2(0, end_mask(first), None)
     plane2(FA - 1, None, end_mask(last))
     axially(start, [plane_up2], [plane_down2], False)

time: 29.9 us -> 28.8 us (0.963)
  Pallas kernels: 29.1 us -> 28 us
    pallas_call x1, Pallas kernels: 26.4 us -> 25.3 us  [local(): pl.pallas_call(functools.partial(advance, n_coarse, n_sector), out_shape=...]
where the time goes in v5:
time: 28.8 us; the launch traced here: 28.7 us
  Pallas kernels  28 us (97%)
  between operations  0.66 us (2%)
    pallas_call x1, Pallas kernels, local(): pl.pallas_call(functools.partial(advance, n_coarse, n_sector), out_shape=...  25.3 us
    pallas_call x1, Pallas kernels, local(): pl.pallas_call(functools.partial(settle, n_coarse), out_shape=jax.ShapeDt...  2.7 us

profile of v5, /device:TPU:1, one launch (start us, length us, event | category | flops | bytes accessed | tf_op | source)
XLA Modules:
  0.0 28.7 jit_solution(3986270180714439755)
XLA Ops:
  0.7 25.3 %advance.1 = (f32[19,824,128]{2,1,0:T(8,128)S(1)}, f32[2,5,48,128]{3,2,1,0:T(8,128)S(1)}, f32[512,128]{1,0:T(8,128)S(1)}) custom-call(f32[19,512,128]{2,1,0:T(8,128)} %bitcast.5, f32[19,2,128]{2,1,0:T(2,128)} %bitcast.7, s32[16,32]{1,0:T(8,128)} %bitcast.8, bf16[3,32,128]{2,1,0:T(8,128)(2,1)} %bitcast.6, bf16[32,128,128]{2,1,0:T(8,128)(2,1)} %mweights_hbm.1, ...), custom_call_target="tpu_custom_call" | custom-call | tf_op jit(solution)/shard_map/advance/pallas_call | solution.py:661
  26.0 2.7 %settle.1 = f32[19,512,128]{2,1,0:T(8,128)} custom-call(f32[19,824,128]{2,1,0:T(8,128)S(1)} %get-tuple-element.8.relaxed, f32[2,5,48,128]{3,2,1,0:T(8,128)S(1)} %get-tuple-element.9.margin, f32[512,128]{1,0:T(8,128)S(1)} %get-tuple-element.10.ghosts), custom_call_target="tpu_custom_call" | custom-call | tf_op jit(solution)/shard_map/settle/pallas_call | solution.py:711

commit v6 on v5

--- a/solution.py
+++ b/solution.py
@@ -478,8 +478,9 @@
     peers = 2 + jnp.where(has_low, 3, 0) + jnp.where(has_high, 3, 0)
     pl.semaphore_wait(barrier, peers)
     ghost_copy.start()
+    start(sides1[0])
     axially(start, small_up, small_down, False)
-    for c in (0, 3, 1, 2):
+    for c in (3, 1, 2):
         start(sides1[c])
     axially(start, [plane_up1], [plane_down1], False)
     lax.fori_loop(1, FA - 1, plane1, 0, unroll=2)
@@ -577,13 +578,13 @@
                 margin_rows(side, slice(8 + a, 16 + a), range(5))
 
     take(0)
-    take(3)
     axially(arrive, small_up, small_down, True)
     for side in range(2):
         margin_rows(side, slice(7, 8), [4])
         margin_rows(side, slice(40, 41), [3])
     edge_rows(0, UP, -1, 7)
     edge_rows(1, DOWN, FA, 40)
+    take(3)
     rim2(0)
     axially(start, [], corners_down, False)
     start(sides2[0])

time: 28.8 us -> 28.7 us (level)
  no operation moved by 1% of the time
where the time goes in v6:
time: 28.7 us; the launch traced here: 28.6 us
  Pallas kernels  27.9 us (97%)
  between operations  0.66 us (2%)
    pallas_call x1, Pallas kernels, local(): pl.pallas_call(functools.partial(advance, n_coarse, n_sector), out_shape=...  25.2 us
    pallas_call x1, Pallas kernels, local(): pl.pallas_call(functools.partial(settle, n_coarse), out_shape=jax.ShapeDt...  2.7 us

profile of v6, /device:TPU:1, one launch (start us, length us, event | category | flops | bytes accessed | tf_op | source)
XLA Modules:
  0.0 28.6 jit_solution(9387209765479325798)
XLA Ops:
  0.7 25.2 %advance.1 = (f32[19,824,128]{2,1,0:T(8,128)S(1)}, f32[2,5,48,128]{3,2,1,0:T(8,128)S(1)}, f32[512,128]{1,0:T(8,128)S(1)}) custom-call(f32[19,512,128]{2,1,0:T(8,128)} %bitcast.5, f32[19,2,128]{2,1,0:T(2,128)} %bitcast.7, s32[16,32]{1,0:T(8,128)} %bitcast.8, bf16[3,32,128]{2,1,0:T(8,128)(2,1)} %bitcast.6, bf16[32,128,128]{2,1,0:T(8,128)(2,1)} %mweights_hbm.1, ...), custom_call_target="tpu_custom_call" | custom-call | tf_op jit(solution)/shard_map/advance/pallas_call | solution.py:662
  25.9 2.7 %settle.1 = f32[19,512,128]{2,1,0:T(8,128)} custom-call(f32[19,824,128]{2,1,0:T(8,128)S(1)} %get-tuple-element.8.relaxed, f32[2,5,48,128]{3,2,1,0:T(8,128)S(1)} %get-tuple-element.9.margin, f32[512,128]{1,0:T(8,128)S(1)} %get-tuple-element.10.ghosts), custom_call_target="tpu_custom_call" | custom-call | tf_op jit(solution)/shard_map/settle/pallas_call | solution.py:712
